TPU v7x, 128 devices: a whole 4x4x4 slice. The times are simulated.
128 devices in a mesh: depth: 16 (over y, x), row: 2 (over core), col: 4 (over z).
Axes of the slice: x: 4, y: 4, z: 4, core: 2. Of those that a mesh axis runs over, the one named last changes fastest.
Arguments:
- inputs: bfloat16 [8192, 6144], P(('depth', 'col'), 'row'), may hold values from -6 to 6
- norm_gain: float32 [6144], P('row'), may hold values from 0.25 to 4, as said below
- w_qkv: bfloat16 [6144, 9216], P(('row', 'depth'), 'col'), as said below
- w_out: bfloat16 [3072, 6144], P(('col', 'depth'), 'row'), may hold values from -0.109375 to 0.109375
- segment_ids: int32 [16, 512], P('depth', 'row'), may hold values from 0 to 33, never falling along the last dimension, each value on 1 to 256 neighbouring positions
- cotangent: bfloat16 [8192, 6144], P(('depth', 'col'), 'row'), may hold values from -6 to 6
Outputs:
- branch_out: bfloat16 [8192, 6144], P(('depth', 'col'), 'row')
- grad_inputs: float32 [8192, 6144], P(('depth', 'col'), 'row')
- grad_gain: float32 [6144], P('row')
- grad_qkv: float32 [6144, 9216], P(('row', 'depth'), 'col')
- grad_out: float32 [3072, 6144], P(('col', 'depth'), 'row')
Inputs may be any that keep to these rules, and one draw needn't show every extreme that they name: `segment_ids`: along each group's row the ids never fall; each image holds 1 to 256 tokens and one holds exactly that many. Attention joins only tokens of one group with equal ids. `norm_gain`: positive gains. `w_qkv`: projection weights of order 6144 ** -0.5.
All inputs are finite; a program needn't handle non-finite values.
Results may differ from a plain program's by a relative error of at most 0.029.
Values may be sent and summed in bfloat16 or wider, within the bound.
A program may use at most 192 MiB of HBM per device.

v0:
```python
import math

import jax
import jax.numpy as jnp
from jax import lax
from jax.sharding import PartitionSpec as P

HD = 128


EPSILON = 1e-06


def head_norm(values):
    centre = values - jnp.mean(values, axis=-1, keepdims=True)
    spread = jnp.mean(centre * centre, axis=-1, keepdims=True)
    return centre * lax.rsqrt(spread + EPSILON)


def shards(inputs, norm_gain, w_qkv, w_out, segment_ids, cotangent):
    row_count = lax.axis_size("row")
    col_count = lax.axis_size("col")
    width = inputs.shape[1] * row_count
    group = inputs.shape[0] * col_count
    height = group // row_count
    heads = w_qkv.shape[1] // (3 * HD)
    score_scale = 1.0 / math.sqrt(HD)
    as_float = inputs.astype(jnp.float32)
    sums, squares = lax.psum(
        (jnp.sum(as_float, axis=1), jnp.sum(as_float * as_float, axis=1)), "row"
    )
    average = (sums / width)[:, None]
    variance = (squares / width)[:, None] - average * average
    inv_scale = lax.rsqrt(variance + EPSILON)
    normed_hat = (as_float - average) * inv_scale
    normed = (normed_hat * norm_gain).astype(jnp.bfloat16)
    qkv_weights = lax.all_gather(w_qkv, "depth", axis=0, tiled=True)
    normed_group = lax.all_gather(normed, "col", axis=0, tiled=True)
    projected_part = jnp.dot(normed_group, qkv_weights, preferred_element_type=jnp.float32)
    own_ids = segment_ids[0]
    group_ids = lax.all_gather(own_ids, "row", axis=0, tiled=True)
    own_rows = (
        lax.psum_scatter(
            projected_part.astype(jnp.bfloat16), "row", scatter_dimension=0, tiled=True
        )
        .astype(jnp.float32)
        .reshape(height, heads, 3, HD)
    )
    queries = own_rows[:, :, 0]
    keys_raw = own_rows[:, :, 1]
    key_own = head_norm(keys_raw).astype(jnp.bfloat16)
    value_own = own_rows[:, :, 2].astype(jnp.bfloat16)
    key_hat, values = (
        lax.all_gather(key_own, "row", axis=0, tiled=True),
        lax.all_gather(value_own, "row", axis=0, tiled=True),
    )
    query_hat = head_norm(queries).astype(jnp.bfloat16)
    same_image = own_ids[:, None] == group_ids[None, :]
    scores = (
        jnp.einsum("qhd,khd->hqk", query_hat, key_hat, preferred_element_type=jnp.float32)
        * score_scale
    )
    weights = jnp.where(same_image[None], jnp.exp(scores), 0.0)
    attn_probs = weights / jnp.sum(weights, axis=-1, keepdims=True)
    probs_low = attn_probs.astype(jnp.bfloat16)
    attended = jnp.einsum(
        "hqk,khd->qhd", probs_low, values, preferred_element_type=jnp.float32
    ).astype(jnp.bfloat16)
    attended_flat = attended.reshape(height, heads * HD)
    attended_group = lax.all_gather(attended_flat, "row", axis=0, tiled=True)
    out_weights = lax.all_gather(w_out, "depth", axis=0, tiled=True)
    branch_part = jnp.dot(attended_group, out_weights, preferred_element_type=jnp.float32)
    branch = lax.psum_scatter(
        branch_part.astype(jnp.bfloat16), "col", scatter_dimension=0, tiled=True
    )
    cot_group = lax.all_gather(cotangent, "col", axis=0, tiled=True)
    attended_part = lax.dot_general(
        cot_group, out_weights, (((1,), (1,)), ((), ())), preferred_element_type=jnp.float32
    )
    grad_attended = lax.psum_scatter(
        attended_part.astype(jnp.bfloat16), "row", scatter_dimension=0, tiled=True
    )
    grad_heads = grad_attended.reshape(height, heads, HD)
    out_part = lax.dot_general(
        attended_group, cot_group, (((0,), (0,)), ((), ())), preferred_element_type=jnp.float32
    )
    grad_out = lax.psum_scatter(
        out_part.astype(jnp.bfloat16), "depth", scatter_dimension=0, tiled=True
    ).astype(jnp.float32)
    out_dot = jnp.sum(grad_heads.astype(jnp.float32) * attended.astype(jnp.float32), axis=-1)
    grad_probs = jnp.einsum("qhd,khd->hqk", grad_heads, values, preferred_element_type=jnp.float32)
    grad_scores = attn_probs * (grad_probs - out_dot.T[:, :, None])
    grad_low = grad_scores.astype(jnp.bfloat16)
    grad_query_hat = (
        jnp.einsum("hqk,khd->qhd", grad_low, key_hat, preferred_element_type=jnp.float32)
        * score_scale
    )
    key_part = (
        jnp.einsum("hqk,qhd->khd", grad_low, query_hat, preferred_element_type=jnp.float32)
        * score_scale
    )
    value_part = jnp.einsum(
        "hqk,qhd->khd", probs_low, grad_heads, preferred_element_type=jnp.float32
    )
    grad_key_hat, grad_values = (
        lax.psum_scatter(
            key_part.astype(jnp.bfloat16), "row", scatter_dimension=0, tiled=True
        ).astype(jnp.float32),
        lax.psum_scatter(
            value_part.astype(jnp.bfloat16), "row", scatter_dimension=0, tiled=True
        ).astype(jnp.float32),
    )
    grad_queries = jax.vjp(head_norm, queries)[1](grad_query_hat)[0]
    grad_keys = jax.vjp(head_norm, keys_raw)[1](grad_key_hat)[0]
    grad_projected = jnp.stack([grad_queries, grad_keys, grad_values], axis=2)
    grad_projected = grad_projected.reshape(height, heads * 3 * HD).astype(jnp.bfloat16)
    grad_group = lax.all_gather(grad_projected, "row", axis=0, tiled=True)
    normed_part = lax.dot_general(
        grad_group, qkv_weights, (((1,), (1,)), ((), ())), preferred_element_type=jnp.float32
    )
    grad_normed = lax.psum_scatter(
        normed_part.astype(jnp.bfloat16), "col", scatter_dimension=0, tiled=True
    ).astype(jnp.float32)
    qkv_part = lax.dot_general(
        normed_group, grad_group, (((0,), (0,)), ((), ())), preferred_element_type=jnp.float32
    )
    grad_qkv = lax.psum_scatter(
        qkv_part.astype(jnp.bfloat16), "depth", scatter_dimension=0, tiled=True
    ).astype(jnp.float32)
    grad_hat = grad_normed * norm_gain
    first_sum, second_sum = lax.psum(
        (jnp.sum(grad_hat, axis=1), jnp.sum(grad_hat * normed_hat, axis=1)), "row"
    )
    grad_inputs = inv_scale * (
        grad_hat - (first_sum / width)[:, None] - normed_hat * (second_sum / width)[:, None]
    )
    grad_gain = lax.psum(jnp.sum(grad_normed * normed_hat, axis=0), ("depth", "col"))
    return (branch, grad_inputs, grad_gain, grad_qkv, grad_out)


def solution(mesh):
    placed = (
        P(("depth", "col"), "row"),
        P("row"),
        P(("row", "depth"), "col"),
        P(("col", "depth"), "row"),
        P("depth", "row"),
        P(("depth", "col"), "row"),
    )
    return jax.shard_map(
        shards,
        mesh=mesh,
        in_specs=placed,
        out_specs=(
            P(("depth", "col"), "row"),
            P(("depth", "col"), "row"),
            P("row"),
            P(("row", "depth"), "col"),
            P(("col", "depth"), "row"),
        ),
        check_vma=False,
    )
```

profile of v0, /device:TPU:0, one launch (start us, length us, event | category | flops | bytes accessed | tf_op | source)
XLA Modules:
  0.0 832.5 jit_solution(10532866923278351033)
XLA Ops:
  8.7 1.4 convert_reduce_fusion
  10.1 2.5 all-reduce.1
  13.2 1.9 fusion.12
  15.7 36.2 %all-gather.14.cloned.1.call-done = bf16[512,3072]{1,0:T(8,128)(2,1)} async-done(((bf16[128,3072]{1,0:T(8,128)(2,1)}), bf16[512,3072]{1,0:T(8,128)(2,1)}) %all-gather.14.cloned.1.call-update) | async-done | bytes 3145744 | tf_op jit(solution)/shard_map/all_gather | solution.py:76
  51.9 56.1 %all-gather.12.cloned.1.call-done = bf16[768,3072]{1,0:T(8,128)(2,1)} async-done(((bf16[48,3072]{1,0:T(8,128)(2,1)}), bf16[768,3072]{1,0:T(8,128)(2,1)}) %all-gather.12.cloned.1.call-update) | async-done | bytes 4718608 | tf_op jit(solution)/shard_map/all_gather | solution.py:71
  108.0 6.8 convolution_convert_fusion.6
  114.9 34.9 %all-gather.8.cloned.1.call-done = bf16[512,3072]{1,0:T(8,128)(2,1)} async-done(((bf16[128,3072]{1,0:T(8,128)(2,1)}), bf16[512,3072]{1,0:T(8,128)(2,1)}) %all-gather.8.cloned.1.call-update) | async-done | bytes 3145744 | tf_op jit(solution)/shard_map/all_gather | solution.py:38
  149.8 99.9 %all-gather.10.cloned.1.call-done = bf16[3072,2304]{1,0:T(8,128)(2,1)} async-done(((bf16[192,2304]{1,0:T(8,128)(2,1)}), bf16[3072,2304]{1,0:T(8,128)(2,1)}) %all-gather.10.cloned.1.call-update) | async-done | bytes 14155792 | tf_op jit(solution)/shard_map/all_gather | solution.py:37
  249.6 14.2 %convolution_convert_fusion.4 = bf16[512,2304]{1,0:T(8,128)(2,1)} fusion(bf16[512,3072]{1,0:T(8,128)(2,1)} %all-gather.8.cloned.1.call-done, bf16[3072,2304]{1,0:T(8,128)(2,1)} %all-gather.10.cloned.1.call-done), kind=kOutput, calls=%fused_computation.4 | convolution fusion | flops 7248936960 | bytes 19660800 | tf_op jit(solution)/shard_map/dot_general | solution.py:39
  264.5 1.8 all-gather.1
  266.3 0.8 broadcast_compare_fusion
  267.1 1.2 copy.24
  268.3 11.0 %reduce-scatter.9.cloned.1.call-done = bf16[256,2304]{1,0:T(8,128)(2,1)} async-done(((bf16[512,2304]{1,0:T(8,128)(2,1)}), bf16[256,2304]{1,0:T(8,128)(2,1)}) %reduce-scatter.9.cloned.1.call-update) | async-done | bytes 1179664 | tf_op jit(solution)/shard_map/reduce_scatter | solution.py:43
  279.3 1.6 copy.21
  280.9 1.4 copy.23
  282.3 2.4 all-gather
  284.7 1.5 reshape.114
  286.7 0.9 multiply_reduce_fusion.3
  288.7 2.5 all_gather.31
  291.3 1.3 fusion.1
  292.6 1.8 multiply_reduce_fusion.1
  294.4 1.3 multiply_convert_fusion
  295.8 1.1 copy-done.2
  296.9 2.0 fusion.14
  299.0 3.8 multiply_reduce_fusion
  302.8 2.1 fusion.15
  305.0 0.7 broadcast_multiply_fusion
  305.7 5.5 reduce-scatter.15.cloned.1.call-done
  311.3 2.6 fusion.24
  313.9 3.1 fusion.21
  317.1 1.7 fusion.22
  318.7 7.9 reduce-scatter.17.cloned.1.call-done
  326.6 1.2 pad_maximum_fusion
  327.9 1.4 copy.32
  329.4 2.4 all_gather.32
  331.8 6.1 convolution_convert_fusion.1
  338.2 6.1 all-gather.16.cloned.1.call-done
  344.3 12.6 %convolution_convert_fusion.2 = bf16[512,3072]{1,0:T(8,128)(2,1)} fusion(bf16[512,2304]{0,1:T(8,128)(2,1)} %all-gather.16.cloned.1.call-done, bf16[3072,2304]{1,0:T(8,128)(2,1)} %all-gather.10.cloned.1.call-done), kind=kOutput, calls=%fused_computation.2 | convolution fusion | flops 7249330176 | bytes 19660800 | tf_op jit(solution)/shard_map/dot_general | solution.py:118
  357.0 13.1 %convolution_convert_fusion = bf16[3072,2304]{1,0:T(8,128)(2,1)} fusion(bf16[512,3072]{1,0:T(8,128)(2,1)} %all-gather.8.cloned.1.call-done, bf16[512,2304]{0,1:T(8,128)(2,1)} %all-gather.16.cloned.1.call-done), kind=kOutput, calls=%fused_computation | convolution fusion | flops 7254835200 | bytes 19660800 | tf_op jit(solution)/shard_map/dot_general | solution.py:124
  370.2 6.7 convolution_convert_fusion.3
  377.0 50.2 %reduce-scatter.23.cloned.1.call-done = bf16[48,3072]{1,0:T(8,128)(2,1)} async-done(((bf16[768,3072]{1,0:T(8,128)(2,1)}), bf16[48,3072]{1,0:T(8,128)(2,1)}) %reduce-scatter.23.cloned.1.call-update) | async-done | bytes 294928 | tf_op jit(solution)/shard_map/reduce_scatter | solution.py:87
  427.1 1.8 convert_element_type.107
  428.9 38.5 %reduce-scatter.19.cloned.1.call-done = bf16[128,3072]{1,0:T(8,128)(2,1)} async-done(((bf16[512,3072]{1,0:T(8,128)(2,1)}), bf16[128,3072]{1,0:T(8,128)(2,1)}) %reduce-scatter.19.cloned.1.call-update) | async-done | bytes 786448 | tf_op jit(solution)/shard_map/reduce_scatter | solution.py:121
  467.4 1.9 fusion.8
  469.4 2.5 all-reduce
  471.8 348.7 %psum.39 = f32[3072]{0:T(1024)} all-reduce(f32[3072]{0:T(1024)S(1)} %get-tuple-element.11), channel_id=1, replica_groups=mesh['depth'=16,'row'=2,'col'=4] {'depth','col'}, use_global_device_ids=true, to_apply=%region_25.26 | all-reduce | flops 3072 | bytes 24576 | tf_op jit(solution)/shard_map/psum | solution.py:137
  820.6 2.9 fusion.6
  823.5 2.5 convert_element_type.105
  (90 shorter events, 5.7 us)
Async XLA Ops:
  7.2 6.0 copy-start
  7.2 44.8 %all-gather.14.cloned.1.call-start = ((), (), s32[]{:S(2)}) async-start(), calls=%async_computation.13 | async-start | bytes 3932160 | tf_op jit(solution)/shard_map/all_gather | solution.py:76
  7.9 100.1 %all-gather.12.cloned.1.call-start = ((), (), s32[]{:S(2)}) async-start(), calls=%async_computation.11 | async-start | bytes 5013504 | tf_op jit(solution)/shard_map/all_gather | solution.py:71
  8.7 141.1 %all-gather.8.cloned.1.call-start = ((), (), s32[]{:S(2)}) async-start(), calls=%async_computation.8 | async-start | bytes 3932160 | tf_op jit(solution)/shard_map/all_gather | solution.py:38
  12.6 0.5 copy-start.16
  12.6 0.6 copy-start.18
  15.1 234.5 %all-gather.10.cloned.1.call-start = ((), (), s32[]{:S(2)}) async-start(), calls=%async_computation.9 | async-start | bytes 15040512 | tf_op jit(solution)/shard_map/all_gather | solution.py:37
  15.7 251.4 %reduce-scatter.13.cloned.1.call-start = ((), (), s32[]{:S(2)}) async-start(), calls=%async_computation.14 | async-start | bytes 1179648 | tf_op jit(solution)/shard_map/reduce_scatter | solution.py:80
  114.9 164.4 %reduce-scatter.9.cloned.1.call-start = ((), (), s32[]{:S(2)}) async-start(), calls=%async_computation.10 | async-start | bytes 3538944 | tf_op jit(solution)/shard_map/reduce_scatter | solution.py:43
  263.9 0.7 copy-start.20
  263.9 47.4 %reduce-scatter.15.cloned.1.call-start = ((), (), s32[]{:S(2)}) async-start(), calls=%async_computation.15 | async-start | bytes 1179648 | tf_op jit(solution)/shard_map/reduce_scatter | solution.py:106
  286.7 4.6 copy-start.8
  287.6 1.1 copy-start.13
  287.6 1.1 copy-start.15
  287.7 0.6 copy-start.6
  291.3 1.3 copy-start.4
  292.6 1.8 copy-start.21
  292.6 1.8 copy-start.23
  295.8 1.1 copy-start.2
  298.9 27.7 %reduce-scatter.17.cloned.1.call-start = ((), (), s32[]{:S(2)}) async-start(), calls=%async_computation.16 | async-start | bytes 1179648 | tf_op jit(solution)/shard_map/reduce_scatter | solution.py:109
  299.0 3.8 copy-start.9
  299.0 3.8 copy-start.22
  299.0 3.8 copy-start.24
  304.9 9.0 %copy-start.14 = (f32[256,6]{0,1:T(8,128)S(1)}, f32[256,6]{0,1:T(8,128)}, u32[]{:S(2)}) copy-start(f32[256,6]{0,1:T(8,128)} %copy-done.13) | copy-start | bytes 18436
  304.9 39.4 %all-gather.16.cloned.1.call-start = ((), (), s32[]{:S(2)}) async-start(), calls=%async_computation.17 | async-start | bytes 3538944 | tf_op jit(solution)/shard_map/all_gather | solution.py:117
  305.7 8.2 copy-start.11
  305.7 8.2 copy-start.12
  311.3 2.6 copy-start.1
  311.3 2.7 copy-start.3
  311.3 5.8 copy-start.7
  327.9 1.5 copy-start.5
  329.3 97.8 %reduce-scatter.23.cloned.1.call-start = ((), (), s32[]{:S(2)}) async-start(), calls=%async_computation.20 | async-start | bytes 5013504 | tf_op jit(solution)/shard_map/reduce_scatter | solution.py:87
  338.0 129.5 %reduce-scatter.19.cloned.1.call-start = ((), (), s32[]{:S(2)}) async-start(), calls=%async_computation.18 | async-start | bytes 3932160 | tf_op jit(solution)/shard_map/reduce_scatter | solution.py:121
  357.0 466.5 %reduce-scatter.21.cloned.1.call-start = ((), (), s32[]{:S(2)}) async-start(), calls=%async_computation.19 | async-start | bytes 15040512 | tf_op jit(solution)/shard_map/reduce_scatter | solution.py:127
  370.2 455.8 %reduce-scatter.11.cloned.1.call-start = ((), (), s32[]{:S(2)}) async-start(), calls=%async_computation.12 | async-start | bytes 3932160 | tf_op jit(solution)/shard_map/reduce_scatter | solution.py:73
  376.9 90.5 %copy-start.10 = (f32[3072]{0:T(1024)S(1)}, f32[3072]{0:T(1024)}, u32[]{:S(2)}) copy-start(f32[3072]{0:T(1024)} %param.7) | copy-start | bytes 36868
  376.9 90.5 %copy-start.17 = (f32[128]{0:T(128)S(1)}, f32[128]{0:T(128)}, u32[]{:S(2)}) copy-start(f32[128]{0:T(128)} %copy-done.16) | copy-start | bytes 1540
  376.9 90.5 %copy-start.19 = (f32[128]{0:T(128)S(1)}, f32[128]{0:T(128)}, u32[]{:S(2)}) copy-start(f32[128]{0:T(128)} %copy-done.18) | copy-start | bytes 1540
Sparse Core Ops, SparseCore 0:
  9.7 42.2 all-gather.13
  54.1 53.9 all-gather.11
  110.3 39.4 all-gather.7
  151.8 97.8 all-gather.9
  252.4 10.4 reduce-scatter.12
  265.3 14.0 reduce-scatter.8
  299.0 12.1 reduce-scatter.14
  314.3 12.2 reduce-scatter.16
  329.4 14.8 all-gather.15
  347.5 79.5 reduce-scatter.22
  429.6 37.8 reduce-scatter.18
  470.8 99.2 reduce-scatter.20
  573.3 38.0 reduce-scatter.10
where the time goes:
time: 833 us; the launch traced here: 832 us
  blocking collectives  363 us (44%)
  waiting for transfers between devices  348 us (42%)
  matrix products  71.9 us (9%)
  other arithmetic  26 us (3%)
  between operations  14.3 us (2%)
  local copies, waits for them, and re-layouts  8.54 us (1%)
    psum x1, blocking collectives, shards(): lax.psum(jnp.sum(grad_normed * normed_hat, axis=0), ('depth', 'col'))  349 us
    all_gather x1, waiting for transfers between devices, shards(): qkv_weights = lax.all_gather(w_qkv, 'depth', axis=0, tiled=True)  99.9 us
    all_gather x1, waiting for transfers between devices, shards(): out_weights = lax.all_gather(w_out, 'depth', axis=0, tiled=True)  56.1 us
    reduce_scatter x1, waiting for transfers between devices, shards(): lax.psum_scatter(out_part.astype(jnp.bfloat16), 'depth', scatter_dimensio...  50.2 us
    reduce_scatter x1, waiting for transfers between devices, shards(): lax.psum_scatter(normed_part.astype(jnp.bfloat16), 'col', scatter_dimensi...  38.5 us
    all_gather x1, waiting for transfers between devices, shards(): cot_group = lax.all_gather(cotangent, 'col', axis=0, tiled=True)  36.2 us
    all_gather x1, waiting for transfers between devices, shards(): normed_group = lax.all_gather(normed, 'col', axis=0, tiled=True)  34.9 us
  transfers between devices with their start and end apart: 13, of which 10 were waited for; matrix products, arithmetic and copies ran while one was open for 11% of the time, Pallas kernels for 0%

commit v1 on v0

v1 whole, which is shorter than its diff:
```python
import math

import jax
import jax.numpy as jnp
from jax import lax
from jax.experimental import pallas as pl
from jax.experimental.pallas import tpu as pltpu
from jax.sharding import PartitionSpec as P

HD = 128
EPSILON = 1e-06
SCALE = 1.0 / math.sqrt(HD)
F32 = jnp.float32
BF16 = jnp.bfloat16
N_SEM = 240


def mm(a, b, ca=1, cb=0):
    return lax.dot_general(a, b, (((ca,), (cb,)), ((), ())), preferred_element_type=F32)


def norm_parts(v):
    centre = v - jnp.mean(v, axis=-1, keepdims=True)
    rs = lax.rsqrt(jnp.mean(centre * centre, axis=-1, keepdims=True) + EPSILON)
    return centre * rs, rs


def norm_back(hat, rs, g):
    dc = rs * (g - hat * jnp.mean(g * hat, axis=-1, keepdims=True))
    return dc - jnp.mean(dc, axis=-1, keepdims=True)


def kernel(
    x_in, gain, w_in, wo_in, ids_row, ids_col, cot_in,
    branch_out, gin_out, gain_out, gqkv_out, gout_out,
    wq, wo, rb, pb, normed, cot, gn, bpart, zb_buf, zg_buf,
    acc, psend, precv, gsend, grecv, gatt, att, gp,
    khat, vals, dk, dv, idr, idc, stat_s, stat_r, avg, inv, sum_s, sum_r,
    gain8, gain_s, gain_r,
    ssem, rsem, lsem, free,
):
    depth = lax.axis_index("depth")
    r = lax.axis_index("row")
    z = lax.axis_index("col")
    y, x = depth // 4, depth % 4
    coord = {"x": x, "y": y, "z": z}
    counter = [0]

    def alloc():
        counter[0] += 1
        return counter[0] - 1

    def dev(ax, i):
        if ax == "x":
            return {"depth": y * 4 + i}
        if ax == "y":
            return {"depth": i * 4 + x}
        if ax == "z":
            return {"col": i}
        return {"row": 1 - r}

    def rcopy(src, dst, k, device):
        return pltpu.make_async_remote_copy(
            src_ref=src, dst_ref=dst, send_sem=ssem.at[k], recv_sem=rsem.at[k],
            device_id=device, device_id_type=pl.DeviceIdType.MESH,
        )

    def nb(ax):
        i = coord[ax]
        return i, lax.rem(i + 1, 4), lax.rem(i + 3, 4), lax.rem(i + 2, 4)

    ring_nbrs = []
    for ax in ("x", "y"):
        _, up, dn, _ = nb(ax)
        ring_nbrs += [dev(ax, up), dev(ax, dn)]
    _, zup, zdn, _ = nb("z")
    all_nbrs = ring_nbrs + [dev("z", zup), dev("z", zdn), dev("r", None)]
    barrier = pltpu.get_barrier_semaphore()
    for d in all_nbrs:
        pl.semaphore_signal(barrier, inc=1, device_id=d, device_id_type=pl.DeviceIdType.MESH)

    local = []

    def lcopy(src, dst):
        c = pltpu.make_async_copy(src, dst, lsem.at[len(local)])
        c.start()
        local.append(c)

    for p in range(4):
        lcopy(wo_in.at[:, pl.ds(p * 768, 768)], wo.at[p, y, x])
    for c in range(3):
        lcopy(w_in.at[:, :, pl.ds(c * 384, 384)], wq.at[c, y, x, :, :, pl.ds(0, 384)])
        lcopy(w_in.at[:, :, pl.ds((3 + c) * 384, 384)], wq.at[c, y, x, :, :, pl.ds(384, 384)])
    lcopy(cot_in, cot.at[z])
    pl.semaphore_wait(barrier, len(all_nbrs))

    def ring_gather(ax, blk, p0, p1):
        i, up, dn, op = nb(ax)
        to_up, to_dn = dev(ax, up), dev(ax, dn)
        k = [alloc() for _ in range(6)]
        sent = []

        def go(b, kk, device):
            c = rcopy(b, b, kk, device)
            c.start()
            sent.append(c)

        def got(b, kk, device):
            rcopy(b, b, kk, device).wait_recv()

        go(blk(p0, i), k[0], to_up)
        go(blk(p1, i), k[1], to_dn)
        go(blk(p1, i), k[2], to_up)
        go(blk(p0, i), k[3], to_dn)
        yield
        got(blk(p0, dn), k[0], to_up)
        go(blk(p0, dn), k[4], to_up)
        got(blk(p1, up), k[1], to_dn)
        go(blk(p1, up), k[5], to_dn)
        yield
        got(blk(p1, dn), k[2], to_up)
        got(blk(p0, up), k[3], to_dn)
        got(blk(p0, op), k[4], to_up)
        got(blk(p1, op), k[5], to_dn)
        for c in sent:
            c.wait_send()
        yield

    def over(ref, f):
        if len(ref.shape) == 3:
            @pl.loop(0, ref.shape[0])
            def _(j):
                f(j)
        else:
            rows = 16

            @pl.loop(0, ref.shape[0] // rows)
            def _(j):
                f(pl.ds(pl.multiple_of(j * rows, rows), rows))

    def add_into(dst, src):
        def f(j):
            dst[j] = (dst[j].astype(F32) + src[j].astype(F32)).astype(BF16)
        over(dst, f)

    def ring_scatter(ax, blk, p0, p1, buf, emit):
        i, up, dn, op = nb(ax)
        to_up, to_dn = dev(ax, up), dev(ax, dn)
        k = [alloc() for _ in range(6)]
        sent = []

        def go(b, n, device):
            c = rcopy(b, buf(n), k[n], device)
            c.start()
            sent.append(c)

        def got(n, device):
            rcopy(buf(n), buf(n), k[n], device).wait_recv()

        go(blk(p0, op), 0, to_up)
        go(blk(p1, op), 1, to_dn)
        go(blk(p1, up), 2, to_up)
        go(blk(p0, dn), 3, to_dn)
        yield
        got(0, to_up)
        add_into(blk(p0, up), buf(0))
        go(blk(p0, up), 4, to_up)
        got(1, to_dn)
        add_into(blk(p1, dn), buf(1))
        go(blk(p1, dn), 5, to_dn)
        yield
        for n, device in ((2, to_up), (3, to_dn), (4, to_up), (5, to_dn)):
            got(n, device)
        emit(p0, blk(p0, i), buf(3), buf(4))
        emit(p1, blk(p1, i), buf(2), buf(5))
        for c in sent:
            c.wait_send()
        yield

    def piece(u, p, yy, xx):
        return wo.at[p, yy, xx] if u == 0 else wq.at[u - 1, yy, xx, p]

    def rowblk(u, p, yy):
        return wo.at[p, yy] if u == 0 else wq.at[u - 1, yy, :, p]

    def colblk(u, p, xx):
        return wo.at[p, :, xx] if u == 0 else wq.at[u - 1, :, xx, p]

    def both(a, b):
        for _ in range(3):
            next(a)
            next(b)
            yield

    def small_gather(u):
        return both(
            ring_gather("x", lambda p, i: piece(u, p, y, i), 0, 1),
            ring_gather("y", lambda p, i: piece(u, p, i, x), 2, 3),
        )

    def big_gather(u):
        return both(
            ring_gather("y", lambda p, i: rowblk(u, p, i), 0, 1),
            ring_gather("x", lambda p, i: colblk(u, p, i), 2, 3),
        )

    def emit_sum(p, own, a, b):
        def f(j):
            own[j] = (own[j].astype(F32) + a[j].astype(F32) + b[j].astype(F32)).astype(BF16)
        over(own, f)

    def big_scatter(u, slot):
        return both(
            ring_scatter("y", lambda p, i: rowblk(u, p, i), 0, 1, lambda n: rb.at[slot, n], emit_sum),
            ring_scatter("x", lambda p, i: colblk(u, p, i), 2, 3, lambda n: rb.at[slot, 6 + n], emit_sum),
        )

    def small_scatter(u):
        def emit(p, own, a, b):
            def f(j):
                total = own[j].astype(F32) + a[j].astype(F32) + b[j].astype(F32)
                if u == 0:
                    gout_out[j, p * 768:(p + 1) * 768] = total
                else:
                    c = u - 1
                    gqkv_out[p, j, c * 384:(c + 1) * 384] = total[:, :384]
                    gqkv_out[p, j, (3 + c) * 384:(4 + c) * 384] = total[:, 384:]
            over(own, f)

        return both(
            ring_scatter("x", lambda p, i: piece(u, p, y, i), 0, 1, lambda n: pb.at[u, n], emit),
            ring_scatter("y", lambda p, i: piece(u, p, i, x), 2, 3, lambda n: pb.at[u, 6 + n], emit),
        )

    def partner_copy(src, dst):
        c = rcopy(src, dst, alloc(), dev("r", None))
        c.start()
        return c

    def ln_stats():
        @pl.loop(0, 4)
        def _(t):
            rows = pl.ds(pl.multiple_of(t * 32, 32), 32)
            v = x_in[rows, :].astype(F32)
            stat_s[rows, :128] = jnp.broadcast_to(jnp.sum(v, axis=1, keepdims=True), (32, 128))
            stat_s[rows, 128:] = jnp.broadcast_to(jnp.sum(v * v, axis=1, keepdims=True), (32, 128))
        return partner_copy(stat_s, stat_r)

    def ln_apply(copy):
        copy.wait()
        total = stat_s[...] + stat_r[...]
        average = total[:, :128] / 6144.0
        variance = total[:, 128:] / 6144.0 - average * average
        avg[...] = average
        inv[...] = lax.rsqrt(variance + EPSILON)

        @pl.loop(0, 2)
        def _(p):
            @pl.loop(0, 2)
            def _(t):
                rows = pl.ds(pl.multiple_of(p * 64 + t * 32, 32), 32)
                v = x_in[rows, :].astype(F32)
                hat = (v - avg[rows, :1]) * inv[rows, :1]
                normed[z, p, pl.ds(pl.multiple_of(t * 32, 32), 32), :] = (hat * gain[...]).astype(BF16)

    def lanes(start, size):
        return pl.ds(pl.multiple_of(start, 128), size)

    def gatt_part(who):
        acc[...] = jnp.zeros_like(acc)

        @pl.loop(0, 4)
        def _(cb):
            left = cot[:, :, :, lanes(cb * 768, 768)].reshape(512, 768)
            right = wo[cb, pl.ds(2 * who, 2)].reshape(384, 768)
            acc[...] += mm(left, right, 1, 1)

    def gatt_first():
        gatt_part(1 - r)
        gsend[...] = acc[...].astype(BF16)
        c = partner_copy(gsend, grecv)
        gatt_part(r)
        return c

    def gatt_last(c):
        c.wait()
        gatt[...] = (acc[...] + grecv[...].astype(F32)).astype(BF16)

    def proj_part(c, who):
        acc[...] = jnp.zeros_like(acc)

        @pl.loop(0, 4)
        def _(k):
            left = normed[:, :, :, lanes(k * 768, 768)].reshape(512, 768)
            right = wq[c, k, :, :, :, lanes(who * 384, 384)].reshape(768, 384)
            acc[...] += mm(left, right)

    def proj_a(c):
        proj_part(c, 1 - r)
        psend[c] = acc[...].astype(BF16)
        return partner_copy(psend.at[c], precv.at[c])

    def proj_b(c):
        proj_part(c, r)

    def attention(c, copy):
        copy.wait()
        acc[...] += precv[c].astype(F32)
        hat, _ = norm_parts(acc[:, 128:256])
        khat[...] = hat.astype(BF16)
        vals[...] = acc[:, 256:].astype(BF16)
        dk[...] = jnp.zeros_like(dk)
        dv[...] = jnp.zeros_like(dv)
        head = lanes((3 * r + c) * 128, 128)
        base = pl.multiple_of(r * 384, 128)

        @pl.loop(0, 4)
        def _(t):
            rows = pl.ds(pl.multiple_of(t * 128, 128), 128)
            qh, rs = norm_parts(acc[rows, :128])
            ql = qh.astype(BF16)
            ids = jnp.concatenate([idr[0], idr[1]], axis=1)
            same = idc[t][:, :1] == ids
            weights = jnp.where(same, jnp.exp(mm(ql, khat[...], 1, 1) * SCALE), 0.0)
            probs = weights * (1.0 / jnp.sum(weights, axis=-1, keepdims=True))
            low = probs.astype(BF16)
            out = mm(low, vals[...]).astype(BF16)
            att[rows, head] = out
            go = gatt[rows, c * 128:(c + 1) * 128]
            dot = jnp.sum(go.astype(F32) * out.astype(F32), axis=-1, keepdims=True)
            gl = (probs * (mm(go, vals[...], 1, 1) - dot)).astype(BF16)
            dq = mm(gl, khat[...]) * SCALE
            dk[...] += mm(gl, ql, 0, 0)
            dv[...] += mm(low, go, 0, 0)
            gp[c, rows, pl.ds(base, 128)] = norm_back(qh, rs, dq).astype(BF16)

        hat, rs = norm_parts(acc[:, 128:256])
        gp[c, :, pl.ds(pl.multiple_of(base + 128, 128), 128)] = norm_back(hat, rs, dk[...] * SCALE).astype(BF16)
        gp[c, :, pl.ds(pl.multiple_of(base + 256, 128), 128)] = dv[...].astype(BF16)
        mine = gp.at[c, :, pl.ds(base, 384)]
        return partner_copy(mine, mine), partner_copy(att.at[:, head], att.at[:, head])

    def weight_grad(c, first, last):
        @pl.loop(first, last)
        def _(f):
            yy, x0 = f // 2, (f % 2) * 2
            right = wq[c, yy, pl.ds(x0, 2)].reshape(384, 768)
            cols = lanes(f * 384, 384)
            part = mm(gp[c], right, 1, 1).reshape(4, 2, 64, 384)
            if c > 0:
                part = part + gn[:, :, :, cols].astype(F32)
            gn[:, :, :, cols] = part.astype(BF16)
            left = normed[:, :, :, cols].reshape(512, 384)
            wq[c, yy, pl.ds(x0, 2)] = mm(left, gp[c], 0, 0).astype(BF16).reshape(2, 4, 48, 768)

    def out_grad():
        @pl.loop(0, 4)
        def _(cb):
            cols = lanes(cb * 768, 768)
            bpart[:, :, :, cols] = mm(att[...], wo[cb].reshape(768, 768)).astype(BF16).reshape(4, 2, 64, 768)
            right = cot[:, :, :, cols].reshape(512, 768)
            wo[cb] = mm(att[...], right, 0, 0).astype(BF16).reshape(4, 4, 48, 768)

    def release(n):
        for d in ring_nbrs:
            pl.semaphore_signal(free.at[n], inc=1, device_id=d, device_id_type=pl.DeviceIdType.MESH)

    def acquire(n):
        pl.semaphore_wait(free.at[n], 4)

    def emit_branch(p, own, a, b):
        def f(j):
            total = own[j].astype(F32) + a[j].astype(F32) + b[j].astype(F32)
            branch_out[p, j] = total.astype(BF16)
        over(own, f)

    def emit_gn(p, own, a, b):
        def f(j):
            gin_out[p, j] = own[j].astype(F32) + a[j].astype(F32) + b[j].astype(F32)
        over(own, f)

    def ln_back_first():
        gain8[...] = jnp.zeros_like(gain8)

        @pl.loop(0, 2)
        def _(p):
            @pl.loop(0, 4)
            def _(t):
                rows = pl.ds(pl.multiple_of(p * 64 + t * 16, 16), 16)
                part = pl.ds(pl.multiple_of(t * 16, 16), 16)
                hat = (x_in[rows, :].astype(F32) - avg[rows, :1]) * inv[rows, :1]
                g = gin_out[p, part, :]
                gh = g * hat
                gain8[...] += gh.reshape(2, 8, 3072).sum(0)
                sum_s[rows, :128] = jnp.broadcast_to(jnp.sum(g * gain[...], axis=1, keepdims=True), (16, 128))
                sum_s[rows, 128:] = jnp.broadcast_to(jnp.sum(gh * gain[...], axis=1, keepdims=True), (16, 128))
        c = partner_copy(sum_s, sum_r)
        gain_s[0] = jnp.sum(gain8[...], axis=0, keepdims=True)
        return c

    def ln_back_last(c):
        c.wait()
        sum_r[...] = (sum_s[...] + sum_r[...]) / 6144.0

        @pl.loop(0, 2)
        def _(p):
            @pl.loop(0, 4)
            def _(t):
                rows = pl.ds(pl.multiple_of(p * 64 + t * 16, 16), 16)
                part = pl.ds(pl.multiple_of(t * 16, 16), 16)
                hat = (x_in[rows, :].astype(F32) - avg[rows, :1]) * inv[rows, :1]
                g = gin_out[p, part, :] * gain[...]
                gin_out[p, part, :] = inv[rows, :1] * (g - sum_r[rows, :1] - hat * sum_r[rows, 128:129])

    def gain_reduce():
        step = 0
        for ax in ("z", "x", "y"):
            i = coord[ax]
            for other in (i + 1 - 2 * (i % 2), 3 - i):
                c = rcopy(gain_s.at[step], gain_r.at[step], alloc(), dev(ax, other))
                c.start()
                yield
                c.wait()
                gain_s[step + 1] = gain_s[step] + gain_r[step]
                step += 1
        gain_out[...] = gain_s[step]
        yield

    sg = [small_gather(u) for u in range(4)]
    bg = [big_gather(u) for u in range(4)]
    z_cot = ring_gather("z", lambda p, i: cot.at[i, p], 0, 1)
    z_normed = ring_gather("z", lambda p, i: normed.at[i, p], 0, 1)

    for c in local:
        c.wait()
    next(sg[0])
    next(z_cot)
    next(sg[1])
    idr[r] = ids_row[...]
    idc[pl.ds(2 * r, 2)] = ids_col[...]
    ids_a = partner_copy(idr.at[r], idr.at[r])
    ids_b = partner_copy(idc.at[pl.ds(2 * r, 2)], idc.at[pl.ds(2 * r, 2)])
    stats = ln_stats()
    next(sg[0])
    next(sg[1])
    ln_apply(stats)
    next(sg[0])
    next(bg[0])
    next(sg[2])
    next(z_cot)
    next(z_normed)
    next(sg[1])
    next(bg[0])
    next(sg[2])
    next(bg[1])
    next(z_cot)
    next(bg[0])
    next(sg[3])
    gcopy = gatt_first()
    next(z_normed)
    next(sg[2])
    next(bg[1])
    next(sg[3])
    next(bg[2])
    gatt_last(gcopy)
    ids_a.wait()
    ids_b.wait()
    next(z_normed)
    next(sg[3])
    next(bg[1])

    pc = proj_a(0)
    next(bg[2])
    proj_b(0)
    next(bg[3])
    ex0 = attention(0, pc)
    next(bg[2])
    for e in ex0:
        e.wait()
    weight_grad(0, 0, 4)
    next(bg[3])
    weight_grad(0, 4, 8)
    rs0, ps0 = big_scatter(1, 0), small_scatter(1)
    rs1, ps1 = big_scatter(2, 1), small_scatter(2)
    rs2, ps2 = big_scatter(0, 0), small_scatter(0)
    rs3, ps3 = big_scatter(3, 1), small_scatter(3)
    next(rs0)
    pc = proj_a(1)
    proj_b(1)
    next(rs0)
    ex1 = attention(1, pc)
    next(bg[3])
    for e in ex1:
        e.wait()
    weight_grad(1, 0, 4)
    weight_grad(1, 4, 8)
    next(rs1)
    next(rs0)
    release(0)
    next(ps0)
    pc = proj_a(2)
    proj_b(2)
    next(rs1)
    next(ps0)
    ex2 = attention(2, pc)
    ex2[1].wait()
    out_grad()
    acquire(0)
    next(rs2)
    z_branch = ring_scatter("z", lambda p, i: bpart.at[i, p], 0, 1, lambda n: zb_buf.at[n], emit_branch)
    z_gn = ring_scatter("z", lambda p, i: gn.at[i, p], 0, 1, lambda n: zg_buf.at[n], emit_gn)
    next(z_branch)
    next(rs1)
    release(1)
    next(ps1)
    next(ps0)
    ex2[0].wait()
    weight_grad(2, 0, 4)
    next(rs2)
    next(ps1)
    weight_grad(2, 4, 8)
    acquire(1)
    next(rs3)
    next(z_branch)
    next(z_gn)
    next(rs2)
    next(ps2)
    next(ps1)
    next(rs3)
    next(ps2)
    next(z_branch)
    next(z_gn)
    next(rs3)
    next(ps3)
    next(ps2)
    next(z_gn)
    back = ln_back_first()
    reduce = gain_reduce()
    next(reduce)
    next(ps3)
    next(reduce)
    ln_back_last(back)
    for _ in range(5):
        next(reduce)
    next(ps3)


def shards(inputs, norm_gain, w_qkv, w_out, segment_ids, cotangent):
    own_ids = segment_ids[0]
    vmem = pl.BlockSpec(memory_space=pltpu.VMEM)
    hbm = pl.BlockSpec(memory_space=pl.ANY)
    V = pltpu.VMEM
    outs = pl.pallas_call(
        kernel,
        out_shape=(
            jax.ShapeDtypeStruct((2, 64, 3072), BF16),
            jax.ShapeDtypeStruct((2, 64, 3072), F32),
            jax.ShapeDtypeStruct((1, 3072), F32),
            jax.ShapeDtypeStruct((4, 48, 2304), F32),
            jax.ShapeDtypeStruct((48, 3072), F32),
        ),
        in_specs=[vmem, vmem, hbm, hbm, vmem, vmem, hbm],
        out_specs=(vmem,) * 5,
        scratch_shapes=[
            V((3, 4, 4, 4, 48, 768), BF16),
            V((4, 4, 4, 48, 768), BF16),
            V((2, 12, 4, 48, 768), BF16),
            V((4, 12, 48, 768), BF16),
            V((4, 2, 64, 3072), BF16),
            V((4, 2, 64, 3072), BF16),
            V((4, 2, 64, 3072), BF16),
            V((4, 2, 64, 3072), BF16),
            V((6, 64, 3072), BF16),
            V((6, 64, 3072), BF16),
            V((512, 384), F32),
            V((3, 512, 384), BF16),
            V((3, 512, 384), BF16),
            V((512, 384), BF16),
            V((512, 384), BF16),
            V((512, 384), BF16),
            V((512, 768), BF16),
            V((3, 512, 768), BF16),
            V((512, 128), BF16),
            V((512, 128), BF16),
            V((512, 128), F32),
            V((512, 128), F32),
            V((2, 1, 256), jnp.int32),
            V((4, 128, 128), jnp.int32),
            V((128, 256), F32),
            V((128, 256), F32),
            V((128, 128), F32),
            V((128, 128), F32),
            V((128, 256), F32),
            V((128, 256), F32),
            V((8, 3072), F32),
            V((7, 1, 3072), F32),
            V((6, 1, 3072), F32),
            pltpu.SemaphoreType.DMA((N_SEM,)),
            pltpu.SemaphoreType.DMA((N_SEM,)),
            pltpu.SemaphoreType.DMA((11,)),
            pltpu.SemaphoreType.REGULAR((2,)),
        ],
        compiler_params=pltpu.CompilerParams(
            collective_id=0, has_side_effects=True, vmem_limit_bytes=62 * 1024 * 1024
        ),
    )(
        inputs,
        norm_gain.reshape(1, 3072),
        w_qkv.reshape(4, 48, 2304),
        w_out,
        own_ids.reshape(1, 256),
        jnp.broadcast_to(own_ids.reshape(2, 128, 1), (2, 128, 128)),
        cotangent.reshape(2, 64, 3072),
    )
    branch, gin, gain, gqkv, gout = outs
    return (
        branch.reshape(128, 3072), gin.reshape(128, 3072), gain.reshape(3072),
        gqkv.reshape(192, 2304), gout,
    )


def solution(mesh):
    placed = (
        P(("depth", "col"), "row"),
        P("row"),
        P(("row", "depth"), "col"),
        P(("col", "depth"), "row"),
        P("depth", "row"),
        P(("depth", "col"), "row"),
    )
    return jax.shard_map(
        shards,
        mesh=mesh,
        in_specs=placed,
        out_specs=(
            P(("depth", "col"), "row"),
            P(("depth", "col"), "row"),
            P("row"),
            P(("row", "depth"), "col"),
            P(("col", "depth"), "row"),
        ),
        check_vma=False,
    )
```

time: 833 us -> 248 us (0.30)
  blocking collectives: 363 us -> 0 us
  waiting for transfers between devices: 348 us -> 0 us
  Pallas kernels: 0 us -> 239 us
  matrix products: 71.9 us -> 0 us
  other arithmetic: 26 us -> 0 us
  between operations: 14.3 us -> 0.65 us
    psum x3 -> x0, blocking collectives: 354 us -> none  [the longest x1 349 us: shards(): lax.psum(jnp.sum(grad_normed * normed_hat, axis=0), ('depth', 'col'))]
    pallas_call x0 -> x1, Pallas kernels: none -> 239 us  [shards(): pl.pallas_call(kernel, out_shape=(jax.ShapeDtypeStruct((2, 64, 3072), BF1...]
    all_gather x5 -> x0, waiting for transfers between devices: 233 us -> none  [the longest x1 99.9 us: shards(): qkv_weights = lax.all_gather(w_qkv, 'depth', axis=0, tiled=True)]
    reduce_scatter x8 -> x0, waiting for transfers between devices: 113 us -> none  [the longest x1 50.2 us: shards(): lax.psum_scatter(out_part.astype(jnp.bfloat16), 'depth', scatter_dimensio...]
    dot_general x12 -> x0, matrix products: 71.9 us -> none  [the longest x1 14.2 us: shards(): jnp.dot(normed_group, qkv_weights, preferred_element_type=jnp.float32)]
    all_gather x4 -> x0, blocking collectives: 9.12 us -> none  [the longest x1 2.55 us: shards(): lax.all_gather(key_own, 'row', axis=0, tiled=True)]
  transfers between devices with their start and end apart: 13 -> 0, of which waited for: 10 -> 0; matrix products, arithmetic and copies ran while one was open for 11% -> 0% of each run, Pallas kernels for 0% -> 0%
where the time goes in v1:
time: 248 us; the launch traced here: 247 us
  Pallas kernels  239 us (96%)
  local copies, waits for them, and re-layouts  7.96 us (3%)
    pallas_call x1, Pallas kernels, shards(): pl.pallas_call(kernel, out_shape=(jax.ShapeDtypeStruct((2, 64, 3072), BF1...  239 us
    unnamed x13, local copies, waits for them, and re-layouts  6.52 us

profile of v1, /device:TPU:0, one launch (start us, length us, event | category | flops | bytes accessed | tf_op | source)
XLA Modules:
  0.0 247.5 jit_solution(1415775927412971992)
XLA Ops:
  0.6 1.4 broadcast_in_dim.8.ids_col
  2.1 238.9 %shard_map.101 = (bf16[2,64,3072]{2,1,0:T(8,128)(2,1)}, f32[2,64,3072]{2,1,0:T(8,128)}, f32[1,3072]{1,0:T(1,128)}, f32[4,48,2304]{2,1,0:T(8,128)}, f32[48,3072]{1,0:T(8,128)}) custom-call(bf16[128,3072]{1,0:T(8,128)(2,1)} %x_in.1, f32[1,3072]{1,0:T(1,128)} %bitcast.13, bf16[4,48,2304]{2,1,0:T(8,128)(2,1)} %bitcast.10, bf16[48,3072]{1,0:T(8,128)(2,1)} %wo_in.1, ...), custom_call_target="tpu_custom_call" | custom-call | tf_op jit(solution)/shard_map/pallas_call | solution.py:553
  240.9 0.0 copy-start.1
  240.9 2.2 copy.16
  243.1 0.0 copy-done.1
  243.1 0.0 copy-start.3
  243.1 0.0 copy-start
  243.1 1.1 copy.17
  244.3 0.0 copy-done.3
  244.3 0.6 copy.18
  244.9 0.3 copy-done
  245.2 0.0 copy-start.2
  245.2 1.2 copy.19
  246.4 0.3 copy-done.2
  246.7 0.8 copy.20
Async XLA Ops:
  240.9 2.2 copy-start.1
  243.1 1.1 copy-start.3
  243.1 2.1 copy-start
  245.2 1.5 copy-start.2

commit v2 on v1

--- a/solution.py
+++ b/solution.py
@@ -31,13 +31,14 @@
 
 
 def kernel(
-    x_in, gain, w_in, wo_in, ids_row, ids_col, cot_in,
-    branch_out, gin_out, gain_out, gqkv_out, gout_out,
+    x_hbm, gain, w_in, wo_in, ids_row, cot_in,
+    branch_hbm, gin_hbm, gain_out, gqkv_hbm, gout_hbm,
+    x_in, branch_out, gin_out, gqkv_out, gout_out,
     wq, wo, rb, pb, normed, cot, gn, bpart, zb_buf, zg_buf,
     acc, psend, precv, gsend, grecv, gatt, att, gp,
     khat, vals, dk, dv, idr, idc, stat_s, stat_r, avg, inv, sum_s, sum_r,
     gain8, gain_s, gain_r,
-    ssem, rsem, lsem, free,
+    ssem, rsem, lsem, osem, free,
 ):
     depth = lax.axis_index("depth")
     r = lax.axis_index("row")
@@ -88,10 +89,11 @@
 
     for p in range(4):
         lcopy(wo_in.at[:, pl.ds(p * 768, 768)], wo.at[p, y, x])
+    lcopy(cot_in, cot.at[z])
+    lcopy(x_hbm, x_in)
     for c in range(3):
         lcopy(w_in.at[:, :, pl.ds(c * 384, 384)], wq.at[c, y, x, :, :, pl.ds(0, 384)])
         lcopy(w_in.at[:, :, pl.ds((3 + c) * 384, 384)], wq.at[c, y, x, :, :, pl.ds(384, 384)])
-    lcopy(cot_in, cot.at[z])
     pl.semaphore_wait(barrier, len(all_nbrs))
 
     def ring_gather(ax, blk, p0, p1):
@@ -237,6 +239,11 @@
         c.start()
         return c
 
+    def id_columns():
+        for t in range(4):
+            row = idr[t // 2][:, (t % 2) * 128:(t % 2 + 1) * 128].astype(F32)
+            idc[t] = jnp.transpose(jnp.broadcast_to(row, (128, 128)))
+
     def ln_stats():
         @pl.loop(0, 4)
         def _(t):
@@ -319,7 +326,7 @@
             rows = pl.ds(pl.multiple_of(t * 128, 128), 128)
             qh, rs = norm_parts(acc[rows, :128])
             ql = qh.astype(BF16)
-            ids = jnp.concatenate([idr[0], idr[1]], axis=1)
+            ids = jnp.concatenate([idr[0], idr[1]], axis=1).astype(F32)
             same = idc[t][:, :1] == ids
             weights = jnp.where(same, jnp.exp(mm(ql, khat[...], 1, 1) * SCALE), 0.0)
             probs = weights * (1.0 / jnp.sum(weights, axis=-1, keepdims=True))
@@ -426,20 +433,33 @@
         gain_out[...] = gain_s[step]
         yield
 
+    outgoing = []
+
+    def leave(src, dst):
+        c = pltpu.make_async_copy(src, dst, osem.at[len(outgoing)])
+        c.start()
+        outgoing.append(c)
+
     sg = [small_gather(u) for u in range(4)]
     bg = [big_gather(u) for u in range(4)]
     z_cot = ring_gather("z", lambda p, i: cot.at[i, p], 0, 1)
     z_normed = ring_gather("z", lambda p, i: normed.at[i, p], 0, 1)
-
-    for c in local:
+    units = (1, 2, 3, 0)
+    rs = [big_scatter(u, k % 2) for k, u in enumerate(units)]
+    ps = [small_scatter(u) for u in units]
+    z_gn = ring_scatter("z", lambda p, i: gn.at[i, p], 0, 1, lambda n: zg_buf.at[n], emit_gn)
+    z_branch = ring_scatter("z", lambda p, i: bpart.at[i, p], 0, 1, lambda n: zb_buf.at[n], emit_branch)
+
+    for c in local[:4]:
         c.wait()
     next(sg[0])
+    local[4].wait()
     next(z_cot)
+    for c in local[5:]:
+        c.wait()
     next(sg[1])
     idr[r] = ids_row[...]
-    idc[pl.ds(2 * r, 2)] = ids_col[...]
     ids_a = partner_copy(idr.at[r], idr.at[r])
-    ids_b = partner_copy(idc.at[pl.ds(2 * r, 2)], idc.at[pl.ds(2 * r, 2)])
     stats = ln_stats()
     next(sg[0])
     next(sg[1])
@@ -457,14 +477,14 @@
     next(bg[0])
     next(sg[3])
     gcopy = gatt_first()
+    ids_a.wait()
+    id_columns()
     next(z_normed)
     next(sg[2])
     next(bg[1])
     next(sg[3])
     next(bg[2])
     gatt_last(gcopy)
-    ids_a.wait()
-    ids_b.wait()
     next(z_normed)
     next(sg[3])
     next(bg[1])
@@ -474,75 +494,89 @@
     proj_b(0)
     next(bg[3])
     ex0 = attention(0, pc)
-    next(bg[2])
     for e in ex0:
         e.wait()
-    weight_grad(0, 0, 4)
-    next(bg[3])
-    weight_grad(0, 4, 8)
-    rs0, ps0 = big_scatter(1, 0), small_scatter(1)
-    rs1, ps1 = big_scatter(2, 1), small_scatter(2)
-    rs2, ps2 = big_scatter(0, 0), small_scatter(0)
-    rs3, ps3 = big_scatter(3, 1), small_scatter(3)
-    next(rs0)
+    weight_grad(0, 0, 8)
+    next(bg[2])
     pc = proj_a(1)
     proj_b(1)
-    next(rs0)
+    next(bg[3])
+    next(rs[0])
     ex1 = attention(1, pc)
-    next(bg[3])
     for e in ex1:
         e.wait()
-    weight_grad(1, 0, 4)
-    weight_grad(1, 4, 8)
-    next(rs1)
-    next(rs0)
-    release(0)
-    next(ps0)
+    weight_grad(1, 0, 8)
+    next(rs[0])
+    next(rs[1])
+    next(bg[3])
     pc = proj_a(2)
     proj_b(2)
-    next(rs1)
-    next(ps0)
     ex2 = attention(2, pc)
+    next(rs[0])
+    release(0)
+    next(ps[0])
+    ex2[0].wait()
+    weight_grad(2, 0, 4)
+    next(rs[1])
+    next(ps[0])
+    weight_grad(2, 4, 8)
+    acquire(0)
+    next(rs[2])
+    next(z_gn)
     ex2[1].wait()
     out_grad()
-    acquire(0)
-    next(rs2)
-    z_branch = ring_scatter("z", lambda p, i: bpart.at[i, p], 0, 1, lambda n: zb_buf.at[n], emit_branch)
-    z_gn = ring_scatter("z", lambda p, i: gn.at[i, p], 0, 1, lambda n: zg_buf.at[n], emit_gn)
     next(z_branch)
-    next(rs1)
+    next(rs[1])
     release(1)
-    next(ps1)
-    next(ps0)
-    ex2[0].wait()
-    weight_grad(2, 0, 4)
-    next(rs2)
-    next(ps1)
-    weight_grad(2, 4, 8)
+    next(ps[1])
+    next(ps[0])
     acquire(1)
-    next(rs3)
-    next(z_branch)
+    next(rs[3])
     next(z_gn)
-    next(rs2)
-    next(ps2)
-    next(ps1)
-    next(rs3)
-    next(ps2)
-    next(z_branch)
+    next(rs[2])
+    next(ps[1])
     next(z_gn)
-    next(rs3)
-    next(ps3)
-    next(ps2)
-    next(z_gn)
+    next(rs[2])
+    next(ps[2])
+    next(ps[1])
     back = ln_back_first()
     reduce = gain_reduce()
     next(reduce)
-    next(ps3)
+    next(z_branch)
+    next(rs[3])
+    next(ps[2])
     next(reduce)
     ln_back_last(back)
-    for _ in range(5):
-        next(reduce)
-    next(ps3)
+    leave(gin_out, gin_hbm)
+    next(reduce)
+    next(reduce)
+    next(rs[3])
+    next(ps[3])
+    next(ps[2])
+    leave(gqkv_out, gqkv_hbm)
+    next(reduce)
+    next(ps[3])
+    next(reduce)
+    next(reduce)
+    next(z_branch)
+    leave(branch_out, branch_hbm)
+    next(ps[3])
+    leave(gout_out, gout_hbm)
+    for c in outgoing:
+        c.wait()
+
+
+def copy_out(*refs):
+    ins, outs, mids, sems = refs[:5], refs[5:10], refs[10:15], refs[15]
+    loads = [pltpu.make_async_copy(ins[k], mids[k], sems.at[0, k]) for k in range(5)]
+    stores = [pltpu.make_async_copy(mids[k], outs[k], sems.at[1, k]) for k in range(5)]
+    for c in loads:
+        c.start()
+    for load, store in zip(loads, stores):
+        load.wait()
+        store.start()
+    for c in stores:
+        c.wait()
 
 
 def shards(inputs, norm_gain, w_qkv, w_out, segment_ids, cotangent):
@@ -559,9 +593,14 @@
             jax.ShapeDtypeStruct((4, 48, 2304), F32),
             jax.ShapeDtypeStruct((48, 3072), F32),
         ),
-        in_specs=[vmem, vmem, hbm, hbm, vmem, vmem, hbm],
-        out_specs=(vmem,) * 5,
+        in_specs=[hbm, vmem, hbm, hbm, vmem, hbm],
+        out_specs=(hbm, hbm, vmem, hbm, hbm),
         scratch_shapes=[
+            V((128, 3072), BF16),
+            V((2, 64, 3072), BF16),
+            V((2, 64, 3072), F32),
+            V((4, 48, 2304), F32),
+            V((48, 3072), F32),
             V((3, 4, 4, 4, 48, 768), BF16),
             V((4, 4, 4, 48, 768), BF16),
             V((2, 12, 4, 48, 768), BF16),
@@ -585,7 +624,7 @@
             V((512, 128), F32),
             V((512, 128), F32),
             V((2, 1, 256), jnp.int32),
-            V((4, 128, 128), jnp.int32),
+            V((4, 128, 128), F32),
             V((128, 256), F32),
             V((128, 256), F32),
             V((128, 128), F32),
@@ -597,7 +636,8 @@
             V((6, 1, 3072), F32),
             pltpu.SemaphoreType.DMA((N_SEM,)),
             pltpu.SemaphoreType.DMA((N_SEM,)),
-            pltpu.SemaphoreType.DMA((11,)),
+            pltpu.SemaphoreType.DMA((12,)),
+            pltpu.SemaphoreType.DMA((4,)),
             pltpu.SemaphoreType.REGULAR((2,)),
         ],
         compiler_params=pltpu.CompilerParams(
@@ -609,10 +649,15 @@
         w_qkv.reshape(4, 48, 2304),
         w_out,
         own_ids.reshape(1, 256),
-        jnp.broadcast_to(own_ids.reshape(2, 128, 1), (2, 128, 128)),
         cotangent.reshape(2, 64, 3072),
     )
-    branch, gin, gain, gqkv, gout = outs
+    branch, gin, gain, gqkv, gout = pl.pallas_call(
+        copy_out,
+        out_shape=tuple(jax.ShapeDtypeStruct(o.shape, o.dtype) for o in outs),
+        in_specs=[hbm] * 5,
+        out_specs=(hbm,) * 5,
+        scratch_shapes=[V(o.shape, o.dtype) for o in outs] + [pltpu.SemaphoreType.DMA((2, 5))],
+    )(*outs)
     return (
         branch.reshape(128, 3072), gin.reshape(128, 3072), gain.reshape(3072),
         gqkv.reshape(192, 2304), gout,

time: 248 us -> 222 us (0.90)
  Pallas kernels: 239 us -> 221 us
  local copies, waits for them, and re-layouts: 7.96 us -> 0 us
    pallas_call x1, Pallas kernels: 239 us -> 217 us  [shards(): pl.pallas_call(kernel, out_shape=(jax.ShapeDtypeStruct((2, 64, 3072), BF1...]
    unnamed x13 -> x0, local copies, waits for them, and re-layouts: 6.52 us -> none
    pallas_call x0 -> x1, Pallas kernels: none -> 3.96 us  [shards(): pl.pallas_call(copy_out, out_shape=tuple((jax.ShapeDtypeStruct(o.shape, o...]
where the time goes in v2:
time: 222 us
  Pallas kernels  221 us (100%)
    pallas_call x1, Pallas kernels, shards(): pl.pallas_call(kernel, out_shape=(jax.ShapeDtypeStruct((2, 64, 3072), BF1...  217 us

profile of v2, /device:TPU:0, one launch (start us, length us, event | category | flops | bytes accessed | tf_op | source)
XLA Modules:
  0.0 221.8 jit_solution(239659412947579836)
XLA Ops:
  0.6 217.0 %shard_map.101 = (bf16[2,64,3072]{2,1,0:T(8,128)(2,1)}, f32[2,64,3072]{2,1,0:T(8,128)}, f32[1,3072]{1,0:T(1,128)}, f32[4,48,2304]{2,1,0:T(8,128)}, f32[48,3072]{1,0:T(8,128)}) custom-call(bf16[128,3072]{1,0:T(8,128)(2,1)} %x_hbm.1, f32[1,3072]{1,0:T(1,128)} %bitcast.9, bf16[4,48,2304]{2,1,0:T(8,128)(2,1)} %bitcast.7, bf16[48,3072]{1,0:T(8,128)(2,1)} %wo_in.1, ...), custom_call_target="tpu_custom_call" | custom-call | tf_op jit(solution)/shard_map/pallas_call | solution.py:587
  217.7 4.0 %shard_map.102 = (bf16[2,64,3072]{2,1,0:T(8,128)(2,1)}, f32[2,64,3072]{2,1,0:T(8,128)}, f32[1,3072]{1,0:T(1,128)}, f32[4,48,2304]{2,1,0:T(8,128)}, f32[48,3072]{1,0:T(8,128)}) custom-call(bf16[2,64,3072]{2,1,0:T(8,128)(2,1)} %get-tuple-element.15.refs_0_, f32[2,64,3072]{2,1,0:T(8,128)} %get-tuple-element.16.refs_1_, f32[1,3072]{1,0:T(1,128)} %get-tuple-element.17.refs_2_, ...), custom_call_target="tpu_custom_call" | custom-call | tf_op jit(solution)/shard_map/pallas_call | solution.py:654

commit v3 on v2

v3 whole, which is shorter than its diff:
```python
import math

import jax
import jax.numpy as jnp
from jax import lax
from jax.experimental import pallas as pl
from jax.experimental.pallas import tpu as pltpu
from jax.sharding import PartitionSpec as P

HD = 128
EPSILON = 1e-06
SCALE = 1.0 / math.sqrt(HD)
F32 = jnp.float32
BF16 = jnp.bfloat16
N_SEM = 240


def mm(a, b, ca=1, cb=0):
    return lax.dot_general(a, b, (((ca,), (cb,)), ((), ())), preferred_element_type=F32)


def norm_parts(v):
    centre = v - jnp.mean(v, axis=-1, keepdims=True)
    rs = lax.rsqrt(jnp.mean(centre * centre, axis=-1, keepdims=True) + EPSILON)
    return centre * rs, rs


def norm_back(hat, rs, g):
    dc = rs * (g - hat * jnp.mean(g * hat, axis=-1, keepdims=True))
    return dc - jnp.mean(dc, axis=-1, keepdims=True)


def kernel(
    x_hbm, gain, w_in, wo_in, ids_row, cot_in,
    branch_hbm, gin_hbm, gain_out, gqkv_hbm, gout_hbm,
    x_in, branch_out, gin_out, gqkv_out, gout_out,
    wq, wo, ra, rbm, pa, pbm, normed, cot, gn, bpart, zb_buf, zg_buf,
    acc, tmp, psend, precv, crecv, gacc, gsend, grecv, gcr, gatt, att, gp,
    khat, vals, dk, dv, idr, idc, stat_s, stat_r, avg, inv, sum_s, sum_r,
    nstage, bstage, gstage, grest, ostage, orecv,
    gain8, gain_s, gain_r,
    ssem, rsem, lsem, osem,
):
    depth = lax.axis_index("depth")
    r = lax.axis_index("row")
    z = lax.axis_index("col")
    y, x = depth // 4, depth % 4
    h, xo = x // 2, x % 2
    coord = {"x": x, "y": y, "z": z}
    counter = [0]

    def alloc():
        counter[0] += 1
        return counter[0] - 1

    def dev(ax, i):
        if ax == "x":
            return {"depth": y * 4 + i}
        if ax == "y":
            return {"depth": i * 4 + x}
        return {"col": i}

    core = {"row": 1 - r}
    pair = {"depth": y * 4 + 3 - x}
    mate = {"depth": y * 4 + x + 1 - 2 * xo}

    def rcopy(src, dst, k, device):
        return pltpu.make_async_remote_copy(
            src_ref=src, dst_ref=dst, send_sem=ssem.at[k], recv_sem=rsem.at[k],
            device_id=device, device_id_type=pl.DeviceIdType.MESH,
        )

    def send(src, dst, device):
        c = rcopy(src, dst, alloc(), device)
        c.start()
        return c

    def nb(ax):
        i = coord[ax]
        return i, lax.rem(i + 1, 4), lax.rem(i + 3, 4), lax.rem(i + 2, 4)

    def lanes(start, size):
        return pl.ds(pl.multiple_of(start, 128), size)

    nbrs = [core, pair, mate]
    for ax in ("y", "z"):
        _, up, dn, _ = nb(ax)
        nbrs += [dev(ax, up), dev(ax, dn)]
    barrier = pltpu.get_barrier_semaphore()
    for d in nbrs:
        pl.semaphore_signal(barrier, inc=1, device_id=d, device_id_type=pl.DeviceIdType.MESH)

    local = []

    def lcopy(src, dst):
        c = pltpu.make_async_copy(src, dst, lsem.at[len(local)])
        c.start()
        local.append(c)

    mine, theirs = h * 1536, (1 - h) * 1536
    lcopy(cot_in.at[:, lanes(mine, 1536)], cot.at[0, z])
    lcopy(x_hbm, x_in)
    for c in range(3):
        lcopy(w_in.at[:, :, pl.ds(c * 384, 384)], wq.at[c, y, xo, :, :, pl.ds(0, 384)])
        lcopy(w_in.at[:, :, pl.ds((3 + c) * 384, 384)], wq.at[c, y, xo, :, :, pl.ds(384, 384)])
    for cb in range(2):
        lcopy(wo_in.at[:, lanes(mine + cb * 768, 768)], wo.at[y, xo, cb])
    pl.semaphore_wait(barrier, len(nbrs))

    def ring_gather(ax, blk, p0, p1, late=False):
        i, up, dn, op = nb(ax)
        to_up, to_dn = dev(ax, up), dev(ax, dn)
        k = [alloc() for _ in range(6)]
        sent = []

        def go(b, kk, device):
            c = rcopy(b, b, kk, device)
            c.start()
            sent.append(c)

        def got(b, kk, device):
            rcopy(b, b, kk, device).wait_recv()

        go(blk(p0, i), k[0], to_up)
        if late:
            go(blk(p0, i), k[3], to_dn)
            yield
        go(blk(p1, i), k[1], to_dn)
        go(blk(p1, i), k[2], to_up)
        if not late:
            go(blk(p0, i), k[3], to_dn)
        yield
        got(blk(p0, dn), k[0], to_up)
        go(blk(p0, dn), k[4], to_up)
        got(blk(p1, up), k[1], to_dn)
        go(blk(p1, up), k[5], to_dn)
        yield
        got(blk(p1, dn), k[2], to_up)
        got(blk(p0, up), k[3], to_dn)
        got(blk(p0, op), k[4], to_up)
        got(blk(p1, op), k[5], to_dn)
        for c in sent:
            c.wait_send()
        yield

    def over(ref, f):
        shape = ref.shape
        if len(shape) == 4:
            @pl.loop(0, shape[0])
            def _(j):
                for k in range(shape[1]):
                    f((j, k))
        elif len(shape) == 3:
            @pl.loop(0, shape[0])
            def _(j):
                f(j)
        else:
            rows = 16

            @pl.loop(0, shape[0] // rows)
            def _(j):
                f(pl.ds(pl.multiple_of(j * rows, rows), rows))

    def add_into(dst, *srcs):
        def f(j):
            total = dst[j].astype(F32)
            for src in srcs:
                total = total + src[j].astype(F32)
            dst[j] = total.astype(BF16)
        over(dst, f)

    def emit_sum(p, own, a, b):
        add_into(own, a, b)

    def ring_scatter(ax, blk, p0, p1, buf, emit, late=False):
        i, up, dn, op = nb(ax)
        to_up, to_dn = dev(ax, up), dev(ax, dn)
        k = [alloc() for _ in range(6)]
        sent = []

        def go(b, n, device):
            c = rcopy(b, buf(n), k[n], device)
            c.start()
            sent.append(c)

        def got(n, device):
            rcopy(buf(n), buf(n), k[n], device).wait_recv()

        go(blk(p0, op), 0, to_up)
        go(blk(p1, op), 1, to_dn)
        if late:
            yield
        go(blk(p1, up), 2, to_up)
        go(blk(p0, dn), 3, to_dn)
        yield
        got(0, to_up)
        add_into(blk(p0, up), buf(0))
        go(blk(p0, up), 4, to_up)
        got(1, to_dn)
        add_into(blk(p1, dn), buf(1))
        go(blk(p1, dn), 5, to_dn)
        yield
        for n, device in ((2, to_up), (3, to_dn), (4, to_up), (5, to_dn)):
            got(n, device)
        emit(p0, blk(p0, i), buf(3), buf(4))
        emit(p1, blk(p1, i), buf(2), buf(5))
        for c in sent:
            c.wait_send()
        yield

    def unit(u):
        return wo if u == 0 else wq.at[u - 1]

    def swap(src, dst):
        c = send(src, dst, mate)
        yield
        yield
        c.wait()
        yield

    def both(a, b):
        for _ in range(3):
            next(a)
            next(b)
            yield

    def small_gather(u):
        w = unit(u)
        block = w.at[y, xo, pl.ds(0, 2)]
        return both(swap(block, block), ring_gather("y", lambda p, i: w.at[i, xo, p], 2, 3))

    def big_gather(u):
        w = unit(u)
        block = w.at[:, xo, pl.ds(2, 2)]
        return both(swap(block, block), ring_gather("y", lambda p, i: w.at[i, :, p], 0, 1))

    def big_scatter(u):
        w = unit(u)

        def column():
            yield from swap_add(w.at[:, 1 - xo, pl.ds(2, 2)], rbm.at[u], w.at[:, xo, pl.ds(2, 2)])
        return both(column(), ring_scatter("y", lambda p, i: w.at[i, :, p], 0, 1, lambda n: ra.at[u, n], emit_sum))

    def swap_add(src, buf, dst):
        c = send(src, buf, mate)
        yield
        yield
        c.wait()
        add_into(dst, buf)
        yield

    def small_scatter(u):
        w = unit(u)

        def place(p, j, total):
            if u == 0 and p < 2:
                gout_out[j, lanes(mine + p * 768, 768)] = total
            elif u == 0:
                ostage[p - 2, j] = total.astype(BF16)
            else:
                c = u - 1
                gqkv_out[p, j, c * 384:(c + 1) * 384] = total[:, :384]
                gqkv_out[p, j, (3 + c) * 384:(4 + c) * 384] = total[:, 384:]

        def emit(p, own, a, b):
            over(own, lambda j: place(p, j, own[j].astype(F32) + a[j].astype(F32) + b[j].astype(F32)))

        def row():
            c = send(w.at[y, 1 - xo, pl.ds(0, 2)], pbm.at[u], mate)
            yield
            yield
            c.wait()
            for p in range(2):
                own = w.at[y, xo, p]
                over(own, lambda j: place(p, j, own[j].astype(F32) + pbm[u, p, j].astype(F32)))
            yield
        return both(row(), ring_scatter("y", lambda p, i: w.at[i, xo, p], 2, 3, lambda n: pa.at[u, n], emit))

    def id_columns():
        for t in range(4):
            row = idr[t // 2][:, (t % 2) * 128:(t % 2 + 1) * 128].astype(F32)
            idc[t] = jnp.transpose(jnp.broadcast_to(row, (128, 128)))

    def ln_stats():
        @pl.loop(0, 4)
        def _(t):
            rows = pl.ds(pl.multiple_of(t * 32, 32), 32)
            v = x_in[rows, :].astype(F32)
            stat_s[rows, :128] = jnp.broadcast_to(jnp.sum(v, axis=1, keepdims=True), (32, 128))
            stat_s[rows, 128:] = jnp.broadcast_to(jnp.sum(v * v, axis=1, keepdims=True), (32, 128))
        return send(stat_s, stat_r, core)

    def ln_apply(copy):
        copy.wait()
        total = stat_s[...] + stat_r[...]
        average = total[:, :128] / 6144.0
        variance = total[:, 128:] / 6144.0 - average * average
        avg[...] = average
        inv[...] = lax.rsqrt(variance + EPSILON)

        def half(which, store):
            @pl.loop(0, 4)
            def _(t):
                rows = pl.ds(pl.multiple_of(t * 32, 32), 32)
                for yy in range(4):
                    cols = lanes(yy * 768 + which * 384, 384)
                    hat = (x_in[rows, cols].astype(F32) - avg[rows, :1]) * inv[rows, :1]
                    store(rows, yy * 384, (hat * gain[:, cols]).astype(BF16))

        def to_pair(rows, at, v):
            nstage[rows, at:at + 384] = v

        def to_own(rows, at, v):
            normed[0, z, rows, at:at + 384] = v

        half(1 - h, to_pair)
        c = send(nstage, normed.at[1, z], pair)
        half(h, to_own)
        return c

    def reduce_out(part, far, own, box_s, box_r, chip_r):
        part(1, 1 - r, far)
        box_s[1] = far[...].astype(BF16)
        a = send(box_s.at[1], box_r.at[1], core)
        part(1, r, far)
        part(0, 1 - r, own)
        box_s[0] = own[...].astype(BF16)
        b = send(box_s.at[0], box_r.at[0], core)
        a.wait()
        box_s[1] = (far[...] + box_r[1].astype(F32)).astype(BF16)
        c = send(box_s.at[1], chip_r, pair)
        part(0, r, own)
        b.wait()
        own[...] += box_r[0].astype(F32)
        return c

    def wo_block(yy, xx, cb):
        if xx < 2:
            return (yy, xx + h * (1 - 2 * xx), 2 * h + cb)
        return (yy, (xx - 2) * h + (3 - xx) * (1 - h), 2 * (1 - h) + cb)

    def gatt_part(slot, who, ref):
        for cb in range(2):
            left = cot[slot, :, :, cb * 768:(cb + 1) * 768].reshape(512, 768)
            right = jnp.concatenate([wo[wo_block(2 * who + k, xx, cb)] for k in range(2) for xx in range(4)], axis=0)
            part = mm(left, right, 1, 1)
            if cb == 0:
                ref[...] = part
            else:
                ref[...] += part

    def gatt_first():
        return reduce_out(gatt_part, tmp, gacc, gsend, grecv, gcr)

    def gatt_last(c):
        c.wait()
        gatt[...] = (gacc[...] + gcr[...].astype(F32)).astype(BF16)

    def proj(c):
        def part(slot, who, ref):
            for k in range(2):
                left = normed[slot, :, :, k * 768:(k + 1) * 768].reshape(512, 768)
                right = wq[c, 2 * k:2 * k + 2, :, :, :, lanes(who * 384, 384)].reshape(768, 384)
                v = mm(left, right)
                if k == 0:
                    ref[...] = v
                else:
                    ref[...] += v
        return reduce_out(part, tmp, acc.at[c], psend.at[c], precv.at[c], crecv.at[c])

    def attention(c):
        a = acc.at[c]
        a[...] += crecv[c].astype(F32)
        hat, _ = norm_parts(a[:, 128:256])
        khat[...] = hat.astype(BF16)
        vals[...] = a[:, 256:].astype(BF16)
        dk[...] = jnp.zeros_like(dk)
        dv[...] = jnp.zeros_like(dv)
        head = lanes((3 * r + c) * 128, 128)
        base = pl.multiple_of(r * 384, 128)

        @pl.loop(0, 4)
        def _(t):
            rows = pl.ds(pl.multiple_of(t * 128, 128), 128)
            qh, rs = norm_parts(a[rows, :128])
            ql = qh.astype(BF16)
            ids = jnp.concatenate([idr[0], idr[1]], axis=1).astype(F32)
            same = idc[t][:, :1] == ids
            weights = jnp.where(same, jnp.exp(mm(ql, khat[...], 1, 1) * SCALE), 0.0)
            probs = weights * (1.0 / jnp.sum(weights, axis=-1, keepdims=True))
            low = probs.astype(BF16)
            out = mm(low, vals[...]).astype(BF16)
            att[0, rows, head] = out
            go = gatt[rows, c * 128:(c + 1) * 128]
            dot = jnp.sum(go.astype(F32) * out.astype(F32), axis=-1, keepdims=True)
            gl = (probs * (mm(go, vals[...], 1, 1) - dot)).astype(BF16)
            dq = mm(gl, khat[...]) * SCALE
            dk[...] += mm(gl, ql, 0, 0)
            dv[...] += mm(low, go, 0, 0)
            gp[c, 0, rows, pl.ds(base, 128)] = norm_back(qh, rs, dq).astype(BF16)

        hat, rs = norm_parts(a[:, 128:256])
        gp[c, 0, :, pl.ds(pl.multiple_of(base + 128, 128), 128)] = norm_back(hat, rs, dk[...] * SCALE).astype(BF16)
        gp[c, 0, :, pl.ds(pl.multiple_of(base + 256, 128), 128)] = dv[...].astype(BF16)
        spots = [(att.at[0, :, head], att.at[1, :, head]), (gp.at[c, 0, :, pl.ds(base, 384)], gp.at[c, 1, :, pl.ds(base, 384)])]
        def move(k):
            near, far = spots[k]
            return send(near, far, pair), far, send(near, near, core)
        return move

    def forward(move):
        chip, far, near = move
        chip.wait_recv()
        return near, chip, send(far, far, core)

    def settle(move):
        for c in (move[0], move[2]):
            c.wait()
        move[1].wait_send()

    def weight_grad(c):
        @pl.loop(0, 4)
        def _(f):
            right = wq[c, f].reshape(384, 768)
            cols = lanes(f * 384, 384)
            both_groups = gp[c].reshape(1024, 768)
            for slot in range(2):
                part = mm(gp[c, slot], right, 1, 1).reshape(4, 128, 384)
                if c > 0:
                    part = part + gn[slot, :, :, cols].astype(F32)
                gn[slot, :, :, cols] = part.astype(BF16)
            left = normed[:, :, :, cols].reshape(1024, 384)
            wq[c, f] = mm(left, both_groups, 0, 0).astype(BF16).reshape(2, 4, 48, 768)

    def out_grad():
        for cb in range(2):
            places = [wo_block(yy, xx, cb) for yy in range(4) for xx in range(4)]

            @pl.loop(0, 2)
            def _(q):
                cols, part = lanes(cb * 768 + q * 384, 384), lanes(q * 384, 384)
                right = jnp.concatenate([wo[(*p, slice(None), part)] for p in places], axis=0)
                for slot in range(2):
                    bpart[slot, :, :, cols] = mm(att[slot], right).astype(BF16).reshape(4, 128, 384)
                heads = att[...].reshape(1024, 768)
                total = mm(heads, cot[:, :, :, cols].reshape(1024, 384), 0, 0).astype(BF16)
                for n, p in enumerate(places):
                    wo[(*p, slice(None), part)] = total[n * 48:(n + 1) * 48]

    def emit_branch(slot, p, own, a, b):
        @pl.loop(0, 4)
        def _(t):
            j = pl.ds(pl.multiple_of(t * 16, 16), 16)
            rows = pl.ds(pl.multiple_of(p * 64 + t * 16, 16), 16)
            total = (own[j].astype(F32) + a[j].astype(F32) + b[j].astype(F32)).astype(BF16)
            if slot == 0:
                branch_out[rows, lanes(mine, 1536)] = total
            else:
                bstage[rows] = total

    def emit_gn(slot, p, own, a, b):
        @pl.loop(0, 4)
        def _(t):
            j = pl.ds(pl.multiple_of(t * 16, 16), 16)
            rows = pl.ds(pl.multiple_of(p * 64 + t * 16, 16), 16)
            total = own[j].astype(F32) + a[j].astype(F32) + b[j].astype(F32)
            if slot == 0:
                for yy in range(4):
                    gin_out[rows, lanes(yy * 768 + h * 384, 384)] = total[:, yy * 384:(yy + 1) * 384]
            else:
                gstage[rows] = total.astype(BF16)

    def gn_rest():
        @pl.loop(0, 8)
        def _(t):
            rows = pl.ds(pl.multiple_of(t * 16, 16), 16)
            for yy in range(4):
                gin_out[rows, lanes(yy * 768 + (1 - h) * 384, 384)] = grest[rows, yy * 384:(yy + 1) * 384].astype(F32)

    def ln_back_first():
        gain8[...] = jnp.zeros_like(gain8)

        @pl.loop(0, 8)
        def _(t):
            rows = pl.ds(pl.multiple_of(t * 16, 16), 16)
            hat = (x_in[rows, :].astype(F32) - avg[rows, :1]) * inv[rows, :1]
            g = gin_out[rows, :]
            gh = g * hat
            gain8[...] += gh.reshape(2, 8, 3072).sum(0)
            sum_s[rows, :128] = jnp.broadcast_to(jnp.sum(g * gain[...], axis=1, keepdims=True), (16, 128))
            sum_s[rows, 128:] = jnp.broadcast_to(jnp.sum(gh * gain[...], axis=1, keepdims=True), (16, 128))
        c = send(sum_s, sum_r, core)
        gain_s[0] = jnp.sum(gain8[...], axis=0, keepdims=True)
        return c

    def ln_back_last(c):
        c.wait()
        sum_r[...] = (sum_s[...] + sum_r[...]) / 6144.0

        @pl.loop(0, 8)
        def _(t):
            rows = pl.ds(pl.multiple_of(t * 16, 16), 16)
            hat = (x_in[rows, :].astype(F32) - avg[rows, :1]) * inv[rows, :1]
            g = gin_out[rows, :] * gain[...]
            gin_out[rows, :] = inv[rows, :1] * (g - sum_r[rows, :1] - hat * sum_r[rows, 128:129])

    def gain_reduce():
        step = 0
        for ax in ("z", "x", "y"):
            i = coord[ax]
            for other in (i + 1 - 2 * (i % 2), 3 - i):
                c = send(gain_s.at[step], gain_r.at[step], dev(ax, other))
                yield
                c.wait()
                gain_s[step + 1] = gain_s[step] + gain_r[step]
                step += 1
        gain_out[...] = gain_s[step]
        yield

    outgoing = []

    def leave(src, dst):
        c = pltpu.make_async_copy(src, dst, osem.at[len(outgoing)])
        c.start()
        outgoing.append(c)

    sg = [small_gather(u) for u in range(4)]
    bg = [big_gather(u) for u in range(4)]
    bs = [big_scatter(u) for u in range(4)]
    ps = [small_scatter(u) for u in range(4)]
    z_cot = ring_gather("z", lambda p, i: cot.at[p, i], 0, 1, late=True)
    z_normed = ring_gather("z", lambda p, i: normed.at[p, i], 0, 1, late=True)
    def z_scatter(array, bufs, slot, emit):
        def half(p):
            return pl.ds(p * 64, 64)
        return ring_scatter(
            "z", lambda p, i: array.at[slot, i, half(p)], 0, 1, lambda n: bufs.at[slot * 6 + n],
            lambda p, own, a, b: emit(slot, p, own, a, b),
        )
    z_gn = [z_scatter(gn, zg_buf, slot, emit_gn) for slot in range(2)]
    z_branch = [z_scatter(bpart, zb_buf, slot, emit_branch) for slot in range(2)]

    wo_sems = [alloc(), alloc()]
    wo_pair = []
    for cb in range(2):
        c = rcopy(wo_in.at[:, lanes(theirs + cb * 768, 768)], wo.at[y, 1 - xo, 2 + cb], wo_sems[cb], pair)
        c.start()
        wo_pair.append(c)
    local[0].wait()
    next(z_cot)
    for c in local[2:8]:
        c.wait()
    next(sg[1])
    local[1].wait()
    idr[r] = ids_row[...]
    ids = send(idr.at[r], idr.at[r], core)
    stats = ln_stats()
    next(sg[2])
    next(sg[1])
    normed_pair = ln_apply(stats)
    next(z_normed)
    next(sg[1])
    next(bg[1])
    next(sg[2])
    for c in local[8:]:
        c.wait()
    for cb in range(2):
        wo_pair[cb].wait_send()
        got = wo.at[y, xo, 2 + cb]
        rcopy(got, got, wo_sems[cb], pair).wait_recv()
    next(sg[0])
    next(bg[1])
    normed_pair.wait()
    next(z_normed)
    cot_pair = send(cot_in.at[:, lanes(theirs, 1536)], cot.at[1, z], pair)
    ids.wait()
    id_columns()
    next(sg[2])
    next(bg[2])
    next(sg[0])
    next(bg[1])
    next(sg[3])
    next(sg[0])
    next(bg[2])
    next(bg[0])
    next(sg[3])
    next(z_normed)
    cot_pair.wait()
    next(z_normed)
    next(z_cot)
    pc0 = proj(0)
    next(bg[2])
    next(bg[0])
    next(sg[3])
    next(bg[3])
    pc1 = proj(1)
    next(z_cot)
    next(bg[0])
    next(z_cot)
    gcopy = gatt_first()
    next(bg[3])
    gatt_last(gcopy)
    next(bg[3])
    pc2 = proj(2)
    pc0.wait()
    move0 = attention(0)
    pc1.wait()
    move1 = attention(1)
    pc2.wait()
    atts = [move0(0), move1(0)]
    move2 = attention(2)
    atts.append(move2(0))
    atts = [forward(m) for m in atts]
    gp0 = move0(1)
    for m in atts:
        settle(m)
    out_grad()
    next(z_branch[1])
    next(z_branch[0])
    next(bs[0])
    gp0 = forward(gp0)
    gp1 = move1(1)
    settle(gp0)
    next(bs[0])
    weight_grad(0)
    next(bs[1])
    gp1 = forward(gp1)
    gp2 = move2(1)
    settle(gp1)
    next(bs[0])
    next(ps[0])
    weight_grad(1)
    next(bs[2])
    next(z_branch[1])
    next(bs[1])
    next(z_branch[0])
    next(ps[0])
    gp2 = forward(gp2)
    settle(gp2)
    weight_grad(2)
    next(z_gn[1])
    next(z_gn[0])
    next(bs[3])
    next(bs[1])
    next(ps[1])
    next(z_branch[1])
    branch_sem = alloc()
    branch_pair = rcopy(bstage, branch_out.at[:, lanes(mine, 1536)], branch_sem, pair)
    branch_pair.start()
    next(z_branch[0])
    next(z_gn[1])
    next(bs[2])
    next(z_gn[0])
    next(ps[0])
    out_pair = send(ostage, orecv, pair)
    next(bs[3])
    next(ps[1])
    next(bs[2])
    next(ps[2])
    branch_pair.wait_send()
    got = branch_out.at[:, lanes(theirs, 1536)]
    rcopy(got, got, branch_sem, pair).wait_recv()
    leave(branch_out, branch_hbm)
    next(z_gn[1])
    gn_pair = send(gstage, grest, pair)
    next(ps[1])
    next(ps[2])
    next(z_gn[0])
    out_pair.wait()
    for cb in range(2):
        gout_out[:, lanes(theirs + cb * 768, 768)] = orecv[cb].astype(F32)
    leave(gout_out, gout_hbm)
    gn_pair.wait()
    gn_rest()
    back = ln_back_first()
    reduce = gain_reduce()
    next(reduce)
    next(bs[3])
    next(ps[3])
    next(reduce)
    ln_back_last(back)
    leave(gin_out, gin_hbm)
    next(reduce)
    next(ps[2])
    next(ps[3])
    next(reduce)
    next(reduce)
    next(ps[3])
    leave(gqkv_out, gqkv_hbm)
    next(reduce)
    next(reduce)
    for c in outgoing:
        c.wait()


def copy_out(*refs):
    ins, outs, mids, sems = refs[:5], refs[5:10], refs[10:15], refs[15]
    loads = [pltpu.make_async_copy(ins[k], mids[k], sems.at[0, k]) for k in range(5)]
    stores = [pltpu.make_async_copy(mids[k], outs[k], sems.at[1, k]) for k in range(5)]
    for c in loads:
        c.start()
    for load, store in zip(loads, stores):
        load.wait()
        store.start()
    for c in stores:
        c.wait()


def shards(inputs, norm_gain, w_qkv, w_out, segment_ids, cotangent):
    own_ids = segment_ids[0]
    vmem = pl.BlockSpec(memory_space=pltpu.VMEM)
    hbm = pl.BlockSpec(memory_space=pl.ANY)
    V = pltpu.VMEM
    outs = pl.pallas_call(
        kernel,
        out_shape=(
            jax.ShapeDtypeStruct((128, 3072), BF16),
            jax.ShapeDtypeStruct((128, 3072), F32),
            jax.ShapeDtypeStruct((1, 3072), F32),
            jax.ShapeDtypeStruct((4, 48, 2304), F32),
            jax.ShapeDtypeStruct((48, 3072), F32),
        ),
        in_specs=[hbm, vmem, hbm, hbm, vmem, hbm],
        out_specs=(hbm, hbm, vmem, hbm, hbm),
        scratch_shapes=[
            V((128, 3072), BF16),
            V((128, 3072), BF16),
            V((128, 3072), F32),
            V((4, 48, 2304), F32),
            V((48, 3072), F32),
            V((3, 4, 2, 4, 48, 768), BF16),
            V((4, 2, 4, 48, 768), BF16),
            V((4, 6, 2, 48, 768), BF16),
            V((4, 4, 2, 48, 768), BF16),
            V((4, 6, 48, 768), BF16),
            V((4, 2, 48, 768), BF16),
            V((2, 4, 128, 1536), BF16),
            V((2, 4, 128, 1536), BF16),
            V((2, 4, 128, 1536), BF16),
            V((2, 4, 128, 1536), BF16),
            V((12, 64, 1536), BF16),
            V((12, 64, 1536), BF16),
            V((3, 512, 384), F32),
            V((512, 384), F32),
            V((3, 2, 512, 384), BF16),
            V((3, 2, 512, 384), BF16),
            V((3, 512, 384), BF16),
            V((512, 384), F32),
            V((2, 512, 384), BF16),
            V((2, 512, 384), BF16),
            V((512, 384), BF16),
            V((512, 384), BF16),
            V((2, 512, 768), BF16),
            V((3, 2, 512, 768), BF16),
            V((512, 128), BF16),
            V((512, 128), BF16),
            V((512, 128), F32),
            V((512, 128), F32),
            V((2, 1, 256), jnp.int32),
            V((4, 128, 128), F32),
            V((128, 256), F32),
            V((128, 256), F32),
            V((128, 128), F32),
            V((128, 128), F32),
            V((128, 256), F32),
            V((128, 256), F32),
            V((128, 1536), BF16),
            V((128, 1536), BF16),
            V((128, 1536), BF16),
            V((128, 1536), BF16),
            V((2, 48, 768), BF16),
            V((2, 48, 768), BF16),
            V((8, 3072), F32),
            V((7, 1, 3072), F32),
            V((6, 1, 3072), F32),
            pltpu.SemaphoreType.DMA((N_SEM,)),
            pltpu.SemaphoreType.DMA((N_SEM,)),
            pltpu.SemaphoreType.DMA((10,)),
            pltpu.SemaphoreType.DMA((4,)),
        ],
        compiler_params=pltpu.CompilerParams(
            collective_id=0, has_side_effects=True, vmem_limit_bytes=62 * 1024 * 1024
        ),
    )(
        inputs,
        norm_gain.reshape(1, 3072),
        w_qkv.reshape(4, 48, 2304),
        w_out,
        own_ids.reshape(1, 256),
        cotangent,
    )
    branch, gin, gain, gqkv, gout = pl.pallas_call(
        copy_out,
        out_shape=tuple(jax.ShapeDtypeStruct(o.shape, o.dtype) for o in outs),
        in_specs=[hbm] * 5,
        out_specs=(hbm,) * 5,
        scratch_shapes=[V(o.shape, o.dtype) for o in outs] + [pltpu.SemaphoreType.DMA((2, 5))],
    )(*outs)
    return (
        branch, gin, gain.reshape(3072),
        gqkv.reshape(192, 2304), gout,
    )


def solution(mesh):
    placed = (
        P(("depth", "col"), "row"),
        P("row"),
        P(("row", "depth"), "col"),
        P(("col", "depth"), "row"),
        P("depth", "row"),
        P(("depth", "col"), "row"),
    )
    return jax.shard_map(
        shards,
        mesh=mesh,
        in_specs=placed,
        out_specs=(
            P(("depth", "col"), "row"),
            P(("depth", "col"), "row"),
            P("row"),
            P(("row", "depth"), "col"),
            P(("col", "depth"), "row"),
        ),
        check_vma=False,
    )
```

time: 222 us -> 215 us (0.968)
  Pallas kernels: 221 us -> 214 us
    pallas_call x1, Pallas kernels: 217 us -> 210 us  [shards(): pl.pallas_call(kernel, out_shape=(jax.ShapeDtypeStruct((128, 3072), BF16)...]
where the time goes in v3:
time: 215 us; the launch traced here: 214 us
  Pallas kernels  214 us (100%)
    pallas_call x1, Pallas kernels, shards(): pl.pallas_call(kernel, out_shape=(jax.ShapeDtypeStruct((128, 3072), BF16)...  210 us

profile of v3, /device:TPU:0, one launch (start us, length us, event | category | flops | bytes accessed | tf_op | source)
XLA Modules:
  0.0 214.3 jit_solution(2359679759793051882)
XLA Ops:
  0.6 209.6 %shard_map.101 = (bf16[128,3072]{1,0:T(8,128)(2,1)}, f32[128,3072]{1,0:T(8,128)}, f32[1,3072]{1,0:T(1,128)}, f32[4,48,2304]{2,1,0:T(8,128)}, f32[48,3072]{1,0:T(8,128)}) custom-call(bf16[128,3072]{1,0:T(8,128)(2,1)} %x_hbm.1, f32[1,3072]{1,0:T(1,128)} %bitcast.5, bf16[4,48,2304]{2,1,0:T(8,128)(2,1)} %bitcast.4, bf16[48,3072]{1,0:T(8,128)(2,1)} %wo_in.1, ...), custom_call_target="tpu_custom_call" | custom-call | tf_op jit(solution)/shard_map/pallas_call | solution.py:714
  210.2 4.0 %shard_map.102 = (bf16[128,3072]{1,0:T(8,128)(2,1)}, f32[128,3072]{1,0:T(8,128)}, f32[1,3072]{1,0:T(1,128)}, f32[4,48,2304]{2,1,0:T(8,128)}, f32[48,3072]{1,0:T(8,128)}) custom-call(bf16[128,3072]{1,0:T(8,128)(2,1)} %get-tuple-element.15.refs_0_, f32[128,3072]{1,0:T(8,128)} %get-tuple-element.16.refs_1_, f32[1,3072]{1,0:T(1,128)} %get-tuple-element.17.refs_2_, ...), custom_call_target="tpu_custom_call" | custom-call | tf_op jit(solution)/shard_map/pallas_call | solution.py:792

commit v4 on v3

--- a/solution.py
+++ b/solution.py
@@ -86,6 +86,7 @@
     for ax in ("y", "z"):
         _, up, dn, _ = nb(ax)
         nbrs += [dev(ax, up), dev(ax, dn)]
+    nbrs += [dev(ax, nb(ax)[3]) for ax in ("x", "y", "z")]
     barrier = pltpu.get_barrier_semaphore()
     for d in nbrs:
         pl.semaphore_signal(barrier, inc=1, device_id=d, device_id_type=pl.DeviceIdType.MESH)
@@ -505,16 +506,21 @@
             gin_out[rows, :] = inv[rows, :1] * (g - sum_r[rows, :1] - hat * sum_r[rows, 128:129])
 
     def gain_reduce():
-        step = 0
-        for ax in ("z", "x", "y"):
-            i = coord[ax]
-            for other in (i + 1 - 2 * (i % 2), 3 - i):
-                c = send(gain_s.at[step], gain_r.at[step], dev(ax, other))
-                yield
-                c.wait()
-                gain_s[step + 1] = gain_s[step] + gain_r[step]
-                step += 1
-        gain_out[...] = gain_s[step]
+        for step, ax in enumerate(("z", "x", "y")):
+            i, up, dn, op = nb(ax)
+            gain_r[step, i] = gain_s[step]
+            copies = []
+            for k, other in ((alloc(), op), (alloc(), up), (alloc(), dn)):
+                c = rcopy(gain_s.at[step], gain_r.at[step, i], k, dev(ax, other))
+                c.start()
+                copies.append((c, k))
+            yield
+            for (c, k), source in zip(copies, (op, dn, up)):
+                c.wait_send()
+                got = gain_r.at[step, source]
+                rcopy(got, got, k, dev(ax, source)).wait_recv()
+            gain_s[step + 1] = (gain_r[step, 0] + gain_r[step, 1]) + (gain_r[step, 2] + gain_r[step, 3])
+        gain_out[...] = gain_s[3]
         yield
 
     outgoing = []
@@ -684,11 +690,8 @@
     next(ps[2])
     next(ps[3])
     next(reduce)
-    next(reduce)
     next(ps[3])
     leave(gqkv_out, gqkv_hbm)
-    next(reduce)
-    next(reduce)
     for c in outgoing:
         c.wait()
 
@@ -771,8 +774,8 @@
             V((2, 48, 768), BF16),
             V((2, 48, 768), BF16),
             V((8, 3072), F32),
-            V((7, 1, 3072), F32),
-            V((6, 1, 3072), F32),
+            V((4, 1, 3072), F32),
+            V((3, 4, 1, 3072), F32),
             pltpu.SemaphoreType.DMA((N_SEM,)),
             pltpu.SemaphoreType.DMA((N_SEM,)),
             pltpu.SemaphoreType.DMA((10,)),

time: 215 us -> 211 us (0.981)
  Pallas kernels: 214 us -> 210 us
    pallas_call x1, Pallas kernels: 210 us -> 206 us  [shards(): pl.pallas_call(kernel, out_shape=(jax.ShapeDtypeStruct((128, 3072), BF16)...]
where the time goes in v4:
time: 211 us
  Pallas kernels  210 us (100%)
    pallas_call x1, Pallas kernels, shards(): pl.pallas_call(kernel, out_shape=(jax.ShapeDtypeStruct((128, 3072), BF16)...  206 us

profile of v4, /device:TPU:0, one launch (start us, length us, event | category | flops | bytes accessed | tf_op | source)
XLA Modules:
  0.0 211.0 jit_solution(13269069734641659479)
XLA Ops:
  0.6 206.2 %shard_map.101 = (bf16[128,3072]{1,0:T(8,128)(2,1)}, f32[128,3072]{1,0:T(8,128)}, f32[1,3072]{1,0:T(1,128)}, f32[4,48,2304]{2,1,0:T(8,128)}, f32[48,3072]{1,0:T(8,128)}) custom-call(bf16[128,3072]{1,0:T(8,128)(2,1)} %x_hbm.1, f32[1,3072]{1,0:T(1,128)} %bitcast.5, bf16[4,48,2304]{2,1,0:T(8,128)(2,1)} %bitcast.4, bf16[48,3072]{1,0:T(8,128)(2,1)} %wo_in.1, ...), custom_call_target="tpu_custom_call" | custom-call | tf_op jit(solution)/shard_map/pallas_call | solution.py:717
  206.9 4.0 %shard_map.102 = (bf16[128,3072]{1,0:T(8,128)(2,1)}, f32[128,3072]{1,0:T(8,128)}, f32[1,3072]{1,0:T(1,128)}, f32[4,48,2304]{2,1,0:T(8,128)}, f32[48,3072]{1,0:T(8,128)}) custom-call(bf16[128,3072]{1,0:T(8,128)(2,1)} %get-tuple-element.15.refs_0_, f32[128,3072]{1,0:T(8,128)} %get-tuple-element.16.refs_1_, f32[1,3072]{1,0:T(1,128)} %get-tuple-element.17.refs_2_, ...), custom_call_target="tpu_custom_call" | custom-call | tf_op jit(solution)/shard_map/pallas_call | solution.py:795
